TPU v7x, 128 devices: a whole 4x4x4 slice. The times are simulated.
128 devices in a mesh: row: 8 (over x_lo, z), col: 16 (over x_hi, y, core).
Axes of the slice: x: 4 (x_hi: 2, x_lo: 2; x = x_hi * 2 + x_lo), y: 4, z: 4, core: 2. Of those that a mesh axis runs over, the one named last changes fastest.
Arguments:
- pair: float32 [512, 512, 128], P('row', 'col')
- token_mask: int32 [512], replicated, may hold values 0 or 1
- norm_gains: float32 [2, 2, 128], replicated, may hold values from 0.1 to 1.9
- norm_biases: float32 [2, 2, 128], replicated, may hold values from -1.5 to 1.5
- in_weights: bfloat16 [2, 128, 640], replicated, may hold values from -0.5 to 0.5
- out_weights: bfloat16 [2, 128, 128], replicated, may hold values from -0.5 to 0.5
Outputs:
- pair_out: float32 [512, 512, 128], P('row', 'col')
Inputs may be any that keep to these rules, and one draw needn't show every extreme that they name: `token_mask`: 1 for a token that takes part, 0 for a padding token.
All inputs are finite; a program needn't handle non-finite values.
Results may differ from a plain program's by a relative error of at most 0.0028.
Values may be sent and summed in bfloat16 or wider, within the bound.
A program may use at most 128 MiB of HBM per device.

v0:
```python
import jax
import jax.numpy as jnp
from jax import lax
from jax.sharding import PartitionSpec as P


def spread(x, axis, root):
    mine = lax.axis_index(axis) == root
    return lax.psum(jnp.where(mine, x, jnp.zeros_like(x)), axis)


def layer_norm(values, norm_gain, norm_bias):
    average = jnp.mean(values, axis=-1, keepdims=True)
    centred = values - average
    variance = jnp.mean(centred * centred, axis=-1, keepdims=True)
    return centred * lax.rsqrt(variance + 1e-05) * norm_gain + norm_bias


def project_pair(source, token_mask, norm_gain, norm_bias, weights_in):
    rows, cols, width = source.shape
    row_mask = lax.dynamic_slice_in_dim(token_mask, lax.axis_index("row") * rows, rows)
    col_mask = lax.dynamic_slice_in_dim(token_mask, lax.axis_index("col") * cols, cols)
    pair_mask = (row_mask[:, None] * col_mask[None, :]).astype(jnp.float32)[:, :, None]
    normed = layer_norm(source, norm_gain, norm_bias).astype(jnp.bfloat16)
    projected = jnp.einsum("rjc,cd->rjd", normed, weights_in, preferred_element_type=jnp.float32)
    left_side = (
        projected[..., :width] * jax.nn.sigmoid(projected[..., 2 * width : 3 * width]) * pair_mask
    ).astype(jnp.bfloat16)
    right_side = (
        projected[..., width : 2 * width]
        * jax.nn.sigmoid(projected[..., 3 * width : 4 * width])
        * pair_mask
    ).astype(jnp.bfloat16)
    out_gate = jax.nn.sigmoid(projected[..., 4 * width :])
    return (left_side, right_side, out_gate)


def finish_pair(source, combined, out_gate, norm_gain, norm_bias, weights_out):
    normed_out = layer_norm(combined, norm_gain, norm_bias).astype(jnp.bfloat16)
    update = jnp.einsum("rjc,cd->rjd", normed_out, weights_out, preferred_element_type=jnp.float32)
    return source + out_gate * update


def body(pair, token_mask, norm_gains, norm_biases, in_weights, out_weights):
    rows, cols, width = pair.shape
    fanout = lax.axis_size("col") // lax.axis_size("row")
    left_side, right_side, out_gate = project_pair(
        pair, token_mask, norm_gains[0, 0], norm_biases[0, 0], in_weights[0]
    )
    left_rows, right_rows = (
        lax.all_gather(left_side, "col", axis=1, tiled=True),
        lax.all_gather(right_side, "col", axis=1, tiled=True),
    )
    col_index = lax.axis_index("col")
    own_rows = lax.dynamic_slice_in_dim(right_rows, col_index % fanout * cols, cols, 0)
    right_mine = spread(own_rows, "row", col_index // fanout)
    combined = jnp.einsum("ikc,jkc->ijc", left_rows, right_mine, preferred_element_type=jnp.float32)
    middle = finish_pair(
        pair, combined, out_gate, norm_gains[0, 1], norm_biases[0, 1], out_weights[0]
    )
    left_side, right_side, out_gate = project_pair(
        middle, token_mask, norm_gains[1, 0], norm_biases[1, 0], in_weights[1]
    )
    left_cols, right_cols = (
        lax.all_gather(left_side, "row", axis=0, tiled=True),
        lax.all_gather(right_side, "row", axis=0, tiled=True),
    )
    row_index = lax.axis_index("row")
    blocks = []
    for portion in range(fanout):
        blocks.append(spread(left_cols, "col", row_index * fanout + portion))
    left_mine = jnp.concatenate(blocks, axis=1)
    combined = jnp.einsum("kic,kjc->ijc", left_mine, right_cols, preferred_element_type=jnp.float32)
    return finish_pair(
        middle, combined, out_gate, norm_gains[1, 1], norm_biases[1, 1], out_weights[1]
    )


def solution(mesh):
    placed = (P("row", "col", None), P(), P(), P(), P(), P())
    return jax.shard_map(
        body, mesh=mesh, in_specs=placed, out_specs=P("row", "col", None), check_vma=False
    )
```

profile of v0, /device:TPU:1, one launch (start us, length us, event | category | flops | bytes accessed | tf_op | source)
XLA Modules:
  0.0 596.6 jit_solution(2313152344391025292)
XLA Ops:
  8.0 1.6 reduce_sum.72
  9.8 1.9 multiply_reduce_fusion.3
  12.7 2.3 fusion.36
  15.1 2.4 copy-done
  17.4 1.6 fusion.33
  19.9 79.9 %all-gather.5.cloned.1.call-done = bf16[64,512,128]{2,1,0:T(8,128)(2,1)} async-done(((bf16[64,32,128]{2,1,0:T(8,128)(2,1)}), bf16[64,512,128]{2,1,0:T(8,128)(2,1)}) %all-gather.5.cloned.1.call-update) | async-done | bytes 8388624 | tf_op jit(solution)/shard_map/all_gather | solution.py:52
  99.8 4.5 dynamic-slice_select_fusion
  104.6 72.1 %all-gather.7.cloned.1.call-done = bf16[64,512,128]{2,1,0:T(8,128)(2,1)} async-done(((bf16[64,32,128]{2,1,0:T(8,128)(2,1)}), bf16[64,512,128]{2,1,0:T(8,128)(2,1)}) %all-gather.7.cloned.1.call-update) | async-done | bytes 8388624 | tf_op jit(solution)/shard_map/all_gather | solution.py:51
  176.7 29.2 %copy.48 = bf16[64,512,128]{0,1,2:T(8,128)(2,1)} copy(bf16[64,512,128]{2,1,0:T(8,128)(2,1)} %all-gather.7.cloned.1.call-done) | data formatting | bytes 16777216 | tf_op jit(solution)/shard_map/all_gather | solution.py:51
  205.9 76.1 %all-reduce.4.cloned.1.call-done = bf16[32,512,128]{2,1,0:T(8,128)(2,1)} async-done(((bf16[32,512,128]{2,1,0:T(8,128)(2,1)}), bf16[32,512,128]{2,1,0:T(8,128)(2,1)}) %all-reduce.4.cloned.1.call-update) | async-done | bytes 4194320 | tf_op jit(solution)/shard_map/psum | solution.py:9
  282.0 8.0 %copy.47 = bf16[32,512,128]{1,0,2:T(8,128)(2,1)} copy(bf16[32,512,128]{2,1,0:T(8,128)(2,1)} %all-reduce.4.cloned.1.call-done) | data formatting | bytes 8388608 | tf_op jit(solution)/shard_map/psum | solution.py:9
  290.0 9.7 %bitcast_reduce_fusion.1 = (f32[64,32]{0,1:T(8,128)S(1)}, f32[128,32,64]{2,1,0:T(8,128)S(1)}) fusion(bf16[32,512,128]{1,0,2:T(8,128)(2,1)} %copy.47, bf16[64,512,128]{0,1,2:T(8,128)(2,1)} %copy.48), kind=kOutput, calls=%fused_computation.10 | convolution fusion | flops 268695552 | bytes 13639680 | tf_op jit(solution)/shard_map/ikc,jkc->ijc/dot_general | solution.py:57
  300.4 1.5 copy.49
  302.0 1.7 fusion.55
  305.8 2.3 copy-done.1
  308.1 1.6 fusion.35
  310.6 50.8 %all-gather.11.cloned.1.call-done = bf16[512,32,128]{2,1,0:T(8,128)(2,1)} async-done(((bf16[64,32,128]{2,1,0:T(8,128)(2,1)}), bf16[512,32,128]{2,1,0:T(8,128)(2,1)}) %all-gather.11.cloned.1.call-update) | async-done | bytes 4194320 | tf_op jit(solution)/shard_map/all_gather | solution.py:65
  361.4 8.6 %copy.54 = bf16[512,32,128]{0,1,2:T(8,128)(2,1)} copy(bf16[512,32,128]{2,1,0:T(8,128)(2,1)} %all-gather.11.cloned.1.call-done) | data formatting | bytes 8388608 | tf_op jit(solution)/shard_map/all_gather | solution.py:65
  370.0 6.1 %broadcast_select_fusion.1 = (bf16[512,32,128]{0,1,2:T(8,128)(2,1)}, bf16[512,32,128]{0,1,2:T(8,128)(2,1)}) fusion(bf16[512,32,128]{0,1,2:T(8,128)(2,1)} %copy.54, pred[]{:T(512)S(6)} %eq.12, pred[]{:T(512)S(6)} %eq.13), kind=kLoop, calls=%fused_computation.6 | loop fusion | flops 4194304 | bytes 12582914 | tf_op jit(solution)/shard_map/jit(_where)/select_n | solution.py:9
  376.1 38.3 %all-gather.9.cloned.1.call-done = bf16[512,32,128]{2,1,0:T(8,128)(2,1)} async-done(((bf16[64,32,128]{2,1,0:T(8,128)(2,1)}), bf16[512,32,128]{2,1,0:T(8,128)(2,1)}) %all-gather.9.cloned.1.call-update) | async-done | bytes 4194320 | tf_op jit(solution)/shard_map/all_gather | solution.py:66
  414.3 8.6 %copy.56 = bf16[512,32,128]{0,1,2:T(8,128)(2,1)} copy(bf16[512,32,128]{2,1,0:T(8,128)(2,1)} %all-gather.9.cloned.1.call-done) | data formatting | bytes 8388608 | tf_op jit(solution)/shard_map/all_gather | solution.py:66
  423.0 154.9 %all-reduce.6.cloned.1.call-done = (bf16[512,32,128]{0,1,2:T(8,128)(2,1)}, bf16[512,32,128]{0,1,2:T(8,128)(2,1)}) async-done(((bf16[512,32,128]{0,1,2:T(8,128)(2,1)}, bf16[512,32,128]{0,1,2:T(8,128)(2,1)}), (bf16[512,32,128]{0,1,2:T(8,128)(2,1)}, bf16[512,32,128]{0,1,2:T(8,128)(2,1)})) %all-reduce.6.cloned.1.call-update) | async-done | bytes 8388624 | tf_op jit(solution)/shard_map/psum | solution.py:9
  577.9 7.0 %bitcast_reduce_fusion = (f32[64,32]{0,1:T(8,128)S(1)}, f32[128,32,64]{2,1,0:T(8,128)S(1)}) fusion(bf16[512,32,128]{0,1,2:T(8,128)(2,1)} %copy.56, bf16[512,32,128]{0,1,2:T(8,128)(2,1)} %get-tuple-element.5, bf16[512,32,128]{0,1,2:T(8,128)(2,1)} %get-tuple-element.6), kind=kOutput, calls=%fused_computation.8 | convolution fusion | flops 285472768 | bytes 13639680 | tf_op jit(solution)/shard_map/kic,kjc->ijc/dot_general | solution.py:73
  587.2 2.6 fusion.4
  (47 shorter events, 9.7 us)
Async XLA Ops:
  6.5 93.3 %all-gather.5.cloned.1.call-start = ((), (), s32[]{:S(2)}) async-start(), calls=%async_computation | async-start | bytes 8912896 | tf_op jit(solution)/shard_map/all_gather | solution.py:52
  15.0 2.4 copy-start
  19.1 157.6 %all-gather.7.cloned.1.call-start = ((), (), s32[]{:S(2)}) async-start(), calls=%async_computation.2 | async-start | bytes 8912896 | tf_op jit(solution)/shard_map/all_gather | solution.py:51
  19.8 262.2 %all-reduce.4.cloned.1.call-start = ((), (), s32[]{:S(2)}) async-start(), calls=%async_computation.1 | async-start | bytes 8388608 | tf_op jit(solution)/shard_map/psum | solution.py:9
  104.4 257.0 %all-gather.11.cloned.1.call-start = ((), (), s32[]{:S(2)}) async-start(), calls=%async_computation.4 | async-start | bytes 4718592 | tf_op jit(solution)/shard_map/all_gather | solution.py:65
  299.6 2.4 copy-start.2
  299.6 2.4 copy-start.4
  300.4 4.3 copy-start.3
  305.8 2.3 copy-start.1
  309.7 104.7 %all-gather.9.cloned.1.call-start = ((), (), s32[]{:S(2)}) async-start(), calls=%async_computation.3 | async-start | bytes 4718592 | tf_op jit(solution)/shard_map/all_gather | solution.py:66
  310.3 267.6 %all-reduce.6.cloned.1.call-start = ((), (), s32[]{:S(2)}) async-start(), calls=%async_computation.5 | async-start | bytes 16777216 | tf_op jit(solution)/shard_map/psum | solution.py:9
Sparse Core Ops, SparseCore 0:
  19.2 80.5 all-gather.4
  102.1 74.5 all-gather.6
  179.2 102.7 all-reduce.3
  309.8 51.5 all-gather.10
  362.9 51.4 all-gather.8
  416.8 161.0 all-reduce.5
where the time goes:
time: 598 us; the launch traced here: 597 us
  waiting for transfers between devices  473 us (79%)
  local copies, waits for them, and re-layouts  65 us (11%)
  matrix products  24.3 us (4%)
  other arithmetic  19.6 us (3%)
  between operations  13.7 us (2%)
    psum x2, waiting for transfers between devices, spread(): return lax.psum(jnp.where(mine, x, jnp.zeros_like(x)), axis)  231 us
    all_gather x1, waiting for transfers between devices, body(): lax.all_gather(right_side, 'col', axis=1, tiled=True)  79.9 us
    all_gather x1, waiting for transfers between devices, body(): lax.all_gather(left_side, 'col', axis=1, tiled=True)  72.1 us
    all_gather x1, waiting for transfers between devices, body(): lax.all_gather(left_side, 'row', axis=0, tiled=True)  50.8 us
    all_gather x1, waiting for transfers between devices, body(): lax.all_gather(right_side, 'row', axis=0, tiled=True)  38.3 us
    all_gather x1, local copies, waits for them, and re-layouts, body(): lax.all_gather(left_side, 'col', axis=1, tiled=True)  29.2 us
  transfers between devices with their start and end apart: 6, of which 6 were waited for; matrix products, arithmetic and copies ran while one was open for 10% of the time, Pallas kernels for 0%

commit v1 on v0

v1 whole, which is shorter than its diff:
```python
import functools

import jax
import jax.numpy as jnp
from jax import lax
from jax.experimental import pallas as pl
from jax.experimental.pallas import tpu as pltpu
from jax.sharding import PartitionSpec as P

MESH = pl.DeviceIdType.MESH
F32, BF16 = jnp.float32, jnp.bfloat16
C = 128
ROWS, COLS = 64, 32
NR, NC = 8, 16
ND = NR * NC
CHUNKS = 16
TN = (((0,), (0,)), ((), ()))
NT = (((1,), (1,)), ((), ()))
NN = (((1,), (0,)), ((), ()))


def dot(a, b, dims):
    return lax.dot_general(a, b, dims, preferred_element_type=F32)


def kernel(pair, mask_smem, mask_vmem, gains, biases, w_in, w_out, out,
           x, normed, gate, w_t, cols, send, recv0, recv1, back, ret0, ret1,
           stage, m_left, m_right, wide,
           send_sems, recv_sems, back_sems, ret_sems):
    r, q = lax.axis_index("row"), lax.axis_index("col")
    me = r * NC + q

    barrier = pltpu.get_barrier_semaphore()

    def greet(o, carry):
        peer = me ^ o
        pl.semaphore_signal(barrier, inc=1, device_id=(peer // NC, peer % NC), device_id_type=MESH)
        return carry

    lax.fori_loop(1, ND, greet, 0)

    for l in range(2):
        w_t[l] = w_in[l, :, : 4 * C].T
        cols[l, 0] = jnp.broadcast_to(gains[2 * l + 1 : 2 * l + 2, :], (C, C)).T
        cols[l, 1] = jnp.broadcast_to(biases[2 * l + 1 : 2 * l + 2, :], (C, C)).T

    low = lax.broadcasted_iota(jnp.int32, (1, C), 1) < ROWS
    pair_rows = mask_vmem[pl.ds(r // 2, 1), :].astype(F32)
    turned = pltpu.roll(pair_rows, ROWS, 1)
    mine = jnp.where(r % 2 == 0, pair_rows, turned)
    row_mask = jnp.where(low, mine, pltpu.roll(mine, ROWS, 1))

    def chunk_mask(s):
        a = mask_smem[q * COLS + s].astype(F32)
        b = mask_smem[q * COLS + CHUNKS + s].astype(F32)
        return row_mask * jnp.where(low, a, b)

    def project(l, t, source):
        mean = jnp.mean(source, axis=-1, keepdims=True)
        centred = source - mean
        var = jnp.mean(centred * centred, axis=-1, keepdims=True)
        g, b = gains[2 * l : 2 * l + 1, :], biases[2 * l : 2 * l + 1, :]
        n = (centred * lax.rsqrt(var + 1e-05) * g + b).astype(BF16)
        normed[pl.ds(t * 256, 256), :] = n
        mask = jnp.concatenate([chunk_mask(2 * t), chunk_mask(2 * t + 1)], axis=1)
        for side in range(2):
            value = dot(w_t[l, side * C : (side + 1) * C, :], n, NT)
            gated = dot(w_t[l, (side + 2) * C : (side + 3) * C, :], n, NT)
            res = value * jax.nn.sigmoid(gated) * mask
            for e in range(2):
                wide[pl.ds(side * 16 + 2 * t + e, C, stride=32), :] = res[:, e * C : (e + 1) * C]

    def send_out(recv, send_sem, recv_sem):
        def group(g, carry):
            base = pl.multiple_of((me ^ (g * 8)) // 8 * 8, 8)
            send[pl.ds(base, 8)] = wide[pl.ds(base * 32, 256), :].astype(BF16).reshape(8, 32, C)

            def one(j, carry):
                peer = me ^ (g * 8 + j)

                @pl.when(peer != me)
                def _():
                    pltpu.make_async_remote_copy(
                        src_ref=send.at[peer], dst_ref=recv.at[me], send_sem=send_sem, recv_sem=recv_sem,
                        device_id=(peer // NC, peer % NC), device_id_type=MESH).start()
                return carry

            return lax.fori_loop(0, 8, one, carry)

        lax.fori_loop(0, ND // 8, group, 0)
        recv[me] = send[me]

    def gates(l):
        def one(t, carry):
            rows = pl.ds(pl.multiple_of(t * 256, 256), 256)
            gate[rows, :] = jax.nn.sigmoid(dot(normed[rows, :], w_in[l, :, 4 * C :], NN))
            return carry
        lax.fori_loop(0, 8, one, 0)

    def wait_all(ref, sem):
        part = ref.at[pl.ds(0, ND - 1)]
        pltpu.make_async_copy(part, part, sem).wait()

    def combine(l, recv, ret, back_sem, ret_sem):
        for rp in range(4):
            def assemble(qq, carry):
                t0 = recv[(2 * rp) * NC + qq].astype(F32)
                t1 = recv[(2 * rp + 1) * NC + qq].astype(F32)
                a = jnp.where(low, t0, pltpu.roll(t1, ROWS, 1)).astype(BF16)
                b = jnp.where(low, pltpu.roll(t0, ROWS, 1), t1).astype(BF16)
                lanes = pl.ds(rp * C, C)
                m_left[qq, 0:16, lanes] = a[0:16]
                m_left[qq, 16:32, lanes] = b[0:16]
                m_right[qq, 0:16, lanes] = a[16:32]
                m_right[qq, 16:32, lanes] = b[16:32]
                return carry
            lax.fori_loop(0, NC, assemble, 0)
        left = m_left[...].reshape(512, 512)
        for qb in range(4):
            if l == 0:
                right = m_right[:, :, qb * C : (qb + 1) * C].reshape(512, C)
                res = dot(right, left, TN)
            else:
                right = m_right[qb * 4 : (qb + 1) * 4].reshape(C, 512)
                res = dot(right, left, NT)
            for qi in range(4):
                for rp in range(4):
                    lanes = slice(rp * C, (rp + 1) * C)
                    x0 = res[qi * 32 : qi * 32 + 16, lanes]
                    x1 = res[qi * 32 + 16 : qi * 32 + 32, lanes]
                    back[2 * rp * NC + qb * 4 + qi] = jnp.where(low, x0, pltpu.roll(x1, ROWS, 1)).astype(BF16)
                    back[(2 * rp + 1) * NC + qb * 4 + qi] = jnp.where(low, pltpu.roll(x0, ROWS, 1), x1).astype(BF16)

        def one(o, carry):
            peer = me ^ o
            pltpu.make_async_remote_copy(
                src_ref=back.at[peer], dst_ref=ret.at[me], send_sem=back_sem, recv_sem=ret_sem,
                device_id=(peer // NC, peer % NC), device_id_type=MESH).start()
            return carry

        lax.fori_loop(1, ND, one, 0)
        ret[me] = back[me]

    def finish(l, t):
        parts = []
        for e in range(2):
            v = stage[pl.ds(2 * t + e, C, stride=16), :]
            mean = jnp.mean(v, axis=0, keepdims=True)
            centred = v - mean
            var = jnp.mean(centred * centred, axis=0, keepdims=True)
            n = (centred * lax.rsqrt(var + 1e-05) * cols[l, 0] + cols[l, 1]).astype(BF16)
            parts.append(dot(n, w_out[l], TN))
        rows = pl.ds(pl.multiple_of(t * 256, 256), 256)
        return x[rows, :] + gate[rows, :] * jnp.concatenate(parts, axis=0)

    def unstage(ret):
        def one(t, carry):
            stage[pl.ds(t * 256, 256), :] = ret[pl.ds(t * 16, 16)].astype(F32).reshape(256, C)
            return carry
        lax.fori_loop(0, 8, one, 0)

    def first(t, carry):
        pieces = [pair[pl.ds(h * 16 + 2 * t + e, ROWS, stride=COLS), :] for e in range(2) for h in range(2)]
        source = jnp.concatenate(pieces, axis=0)
        x[pl.ds(pl.multiple_of(t * 256, 256), 256), :] = source
        project(0, t, source)
        return carry

    lax.fori_loop(0, 8, first, 0)
    pl.semaphore_wait(barrier, ND - 1)
    send_out(recv0, send_sems.at[0], recv_sems.at[0])
    gates(0)
    wait_all(recv0, recv_sems.at[0])
    combine(0, recv0, ret0, back_sems.at[0], ret_sems.at[0])
    wait_all(ret0, ret_sems.at[0])
    wait_all(send, send_sems.at[0])
    wait_all(back, back_sems.at[0])
    unstage(ret0)

    def second(t, carry):
        source = finish(0, t)
        x[pl.ds(pl.multiple_of(t * 256, 256), 256), :] = source
        project(1, t, source)
        return carry

    lax.fori_loop(0, 8, second, 0)
    send_out(recv1, send_sems.at[1], recv_sems.at[1])
    gates(1)
    wait_all(recv1, recv_sems.at[1])
    combine(1, recv1, ret1, back_sems.at[1], ret_sems.at[1])
    wait_all(ret1, ret_sems.at[1])
    wait_all(send, send_sems.at[1])
    wait_all(back, back_sems.at[1])
    unstage(ret1)

    def third(t, carry):
        res = finish(1, t)
        for e in range(2):
            for h in range(2):
                at = (2 * e + h) * ROWS
                out[pl.ds(h * 16 + 2 * t + e, ROWS, stride=COLS), :] = res[at : at + ROWS]
        return carry

    lax.fori_loop(0, 8, third, 0)


def body(pair, token_mask, norm_gains, norm_biases, in_weights, out_weights):
    vmem = pl.BlockSpec(memory_space=pltpu.VMEM)
    res = pl.pallas_call(
        kernel,
        out_shape=jax.ShapeDtypeStruct((ROWS * COLS, C), F32),
        in_specs=[vmem, pl.BlockSpec(memory_space=pltpu.SMEM)] + [vmem] * 5,
        out_specs=vmem,
        scratch_shapes=[
            pltpu.VMEM((2048, C), F32),
            pltpu.VMEM((2048, C), BF16),
            pltpu.VMEM((2048, C), F32),
            pltpu.VMEM((2, 4 * C, C), BF16),
            pltpu.VMEM((2, 2, C, C), F32),
            pltpu.VMEM((ND, 32, C), BF16),
            pltpu.VMEM((ND, 32, C), BF16),
            pltpu.VMEM((ND, 32, C), BF16),
            pltpu.VMEM((ND, 16, C), BF16),
            pltpu.VMEM((ND, 16, C), BF16),
            pltpu.VMEM((ND, 16, C), BF16),
            pltpu.VMEM((2048, C), F32),
            pltpu.VMEM((NC, 32, 512), BF16),
            pltpu.VMEM((NC, 32, 512), BF16),
            pltpu.VMEM((4096, C), F32),
            pltpu.SemaphoreType.DMA((2,)),
            pltpu.SemaphoreType.DMA((2,)),
            pltpu.SemaphoreType.DMA((2,)),
            pltpu.SemaphoreType.DMA((2,)),
        ],
        compiler_params=pltpu.CompilerParams(
            collective_id=0, has_side_effects=True, vmem_limit_bytes=48 << 20),
    )(
        pair.reshape(ROWS * COLS, C), token_mask, token_mask.reshape(4, C),
        norm_gains.reshape(4, C), norm_biases.reshape(4, C), in_weights, out_weights,
    )
    return res.reshape(ROWS, COLS, C)


def solution(mesh):
    placed = (P("row", "col", None), P(), P(), P(), P(), P())
    return jax.shard_map(
        body, mesh=mesh, in_specs=placed, out_specs=P("row", "col", None), check_vma=False
    )
```

time: 598 us -> 95.1 us (0.16)
  waiting for transfers between devices: 473 us -> 0 us
  Pallas kernels: 0 us -> 90.2 us
  local copies, waits for them, and re-layouts: 65 us -> 4.72 us
  matrix products: 24.3 us -> 0 us
  other arithmetic: 19.6 us -> 0 us
  between operations: 13.7 us -> 0.02 us
    all_gather x4 -> x0, waiting for transfers between devices: 241 us -> none  [the longest x1 79.9 us: body(): lax.all_gather(right_side, 'col', axis=1, tiled=True)]
    psum x2 -> x0, waiting for transfers between devices: 231 us -> none  [spread(): return lax.psum(jnp.where(mine, x, jnp.zeros_like(x)), axis)]
    pallas_call x0 -> x1, Pallas kernels: none -> 90.2 us  [body(): pl.pallas_call(kernel, out_shape=jax.ShapeDtypeStruct((ROWS * COLS, C), F...]
    all_gather x3 -> x0, local copies, waits for them, and re-layouts: 46.3 us -> none  [the longest x1 29.2 us: body(): lax.all_gather(left_side, 'col', axis=1, tiled=True)]
    dot_general x6 -> x0, matrix products: 24.3 us -> none  [the longest x1 9.67 us: body(): jnp.einsum('ikc,jkc->ijc', left_rows, right_mine, preferred_element_type=...]
    select_n x2 -> x0, other arithmetic: 10.6 us -> none  [spread(): return lax.psum(jnp.where(mine, x, jnp.zeros_like(x)), axis)]
    psum x1 -> x0, local copies, waits for them, and re-layouts: 7.98 us -> none  [spread(): return lax.psum(jnp.where(mine, x, jnp.zeros_like(x)), axis)]
  transfers between devices with their start and end apart: 6 -> 0, of which waited for: 6 -> 0; matrix products, arithmetic and copies ran while one was open for 10% -> 0% of each run, Pallas kernels for 0% -> 0%
where the time goes in v1:
time: 95.1 us; the launch traced here: 94.9 us
  Pallas kernels  90.2 us (95%)
  local copies, waits for them, and re-layouts  4.72 us (5%)
    pallas_call x1, Pallas kernels, body(): pl.pallas_call(kernel, out_shape=jax.ShapeDtypeStruct((ROWS * COLS, C), F...  90.2 us
    unnamed x13, local copies, waits for them, and re-layouts  4.72 us

profile of v1, /device:TPU:1, one launch (start us, length us, event | category | flops | bytes accessed | tf_op | source)
XLA Modules:
  0.0 94.9 jit_solution(12729567707413306266)
XLA Ops:
  0.0 0.0 copy-start.5
  0.0 0.0 copy-start.4
  0.0 0.0 copy-start.3
  0.0 0.7 copy-done.5
  0.7 0.0 copy-done.4
  0.7 0.0 copy-done.3
  0.7 0.0 copy-start
  0.7 1.2 %copy-done = f32[64,32,128]{2,1,0:T(8,128)S(1)} copy-done((f32[64,32,128]{2,1,0:T(8,128)S(1)}, f32[64,32,128]{2,1,0:T(8,128)}, u32[]{:S(2)}) %copy-start) | copy-done | bytes 1048600
  1.9 0.0 copy-start.1
  1.9 1.0 %copy-done.1 = bf16[2,128,640]{2,1,0:T(8,128)(2,1)S(1)} copy-done((bf16[2,128,640]{2,1,0:T(8,128)(2,1)S(1)}, bf16[2,128,640]{2,1,0:T(8,128)(2,1)}, u32[]{:S(2)}) %copy-start.1) | copy-done | bytes 327704
  2.9 0.0 copy-start.2
  2.9 0.8 copy-done.2
  3.8 90.2 %shard_map.64 = f32[2048,128]{1,0:T(8,128)S(1)} custom-call(f32[2048,128]{1,0:T(8,128)S(1)} %bitcast.6, s32[512]{0:T(512)S(1)} %copy-done.3, s32[4,128]{1,0:T(4,128)S(1)} %bitcast.7, f32[4,128]{1,0:T(4,128)S(1)} %bitcast.8, f32[4,128]{1,0:T(4,128)S(1)} %bitcast.9, bf16[2,128,640]{2,1,0:T(8,128)(2,1)S(1)} %copy-done.1, bf16[2,128,128]{2,1,0:T(8,128)(2,1)S(1)} %copy-done.2), custom_call_target="tpu_custom_call" | custom-call | tf_op jit(solution)/shard_map/pallas_call | solution.py:209
  93.9 1.0 %copy.8 = f32[64,32,128]{2,1,0:T(8,128)} copy(f32[64,32,128]{2,1,0:T(8,128)S(1)} %bitcast.5) | data formatting | bytes 2097152
Async XLA Ops:
  0.0 0.7 copy-start.5
  0.0 0.7 copy-start.4
  0.0 0.7 copy-start.3
  0.7 1.2 %copy-start = (f32[64,32,128]{2,1,0:T(8,128)S(1)}, f32[64,32,128]{2,1,0:T(8,128)}, u32[]{:S(2)}) copy-start(f32[64,32,128]{2,1,0:T(8,128)} %param.6) | copy-start | bytes 3145732
  1.9 1.0 %copy-start.1 = (bf16[2,128,640]{2,1,0:T(8,128)(2,1)S(1)}, bf16[2,128,640]{2,1,0:T(8,128)(2,1)}, u32[]{:S(2)}) copy-start(bf16[2,128,640]{2,1,0:T(8,128)(2,1)} %w_in.1) | copy-start | bytes 983044
  2.9 0.8 copy-start.2

commit v2 on v1

v2 whole, which is shorter than its diff:
```python
import jax
import jax.numpy as jnp
from jax import lax
from jax.experimental import pallas as pl
from jax.experimental.pallas import tpu as pltpu
from jax.sharding import PartitionSpec as P

MESH = pl.DeviceIdType.MESH
F32, BF16 = jnp.float32, jnp.bfloat16
C = 128
ROWS, COLS = 64, 32
NR, NC = 8, 16
ND = NR * NC
CHUNKS = 16
GROUPS = 4
MEMBERS = ND // GROUPS
TN = (((0,), (0,)), ((), ()))
NT = (((1,), (1,)), ((), ()))
NN = (((1,), (0,)), ((), ()))


def dot(a, b, dims):
    return lax.dot_general(a, b, dims, preferred_element_type=F32)


def place(device):
    return (device // NC, device % NC)


def group_offset(g, k):
    k = (7 * k) % MEMBERS
    return (g // 2) * 64 + (g % 2) * 16 + (k // 16) * 32 + k % 16


def kernel(pair_hbm, mask_smem, mask_vmem, gains, biases, w_in_hbm, w_out_hbm, out,
           pair, w_in, w_out, x, normed, gate, w_t, cols, send, recv0, recv1, back, ret0, ret1,
           stage, m_left, m_right, wide,
           load_sems, send_sems, recv_sems, back_sems, ret_sems):
    r, q = lax.axis_index("row"), lax.axis_index("col")
    me = r * NC + q

    barrier = pltpu.get_barrier_semaphore()

    def greet(i, carry):
        i = ND - 1 - i
        hi, lo = i // 16, 15 - i % 16
        o = (hi // 4) * 32 + (hi // 2 % 2) * 8 + (hi % 2) * 4
        o = o + (lo // 8) * 64 + (lo // 4 % 2) * 16 + lo % 4

        @pl.when(o != 0)
        def _():
            pl.semaphore_signal(barrier, inc=1, device_id=place(me ^ o), device_id_type=MESH)
        return carry

    loads = [
        pltpu.make_async_copy(w_in_hbm, w_in, load_sems.at[0]),
        pltpu.make_async_copy(pair_hbm, pair, load_sems.at[1]),
        pltpu.make_async_copy(w_out_hbm, w_out, load_sems.at[2]),
    ]
    for load in loads:
        load.start()
    lax.fori_loop(0, ND, greet, 0)

    low = lax.broadcasted_iota(jnp.int32, (1, C), 1) < ROWS
    pair_rows = mask_vmem[pl.ds(r // 2, 1), :].astype(F32)
    turned = pltpu.roll(pair_rows, ROWS, 1)
    mine = jnp.where(r % 2 == 0, pair_rows, turned)
    row_mask = jnp.where(low, mine, pltpu.roll(mine, ROWS, 1))

    def chunk_mask(s):
        a = mask_smem[q * COLS + s].astype(F32)
        b = mask_smem[q * COLS + CHUNKS + s].astype(F32)
        return row_mask * jnp.where(low, a, b)

    for l in range(2):
        cols[l, 0] = jnp.broadcast_to(gains[2 * l + 1 : 2 * l + 2, :], (C, C)).T
        cols[l, 1] = jnp.broadcast_to(biases[2 * l + 1 : 2 * l + 2, :], (C, C)).T
    loads[0].wait()
    for l in range(2):
        w_t[l] = w_in[l, :, : 4 * C].T
    loads[1].wait()
    loads[2].wait()

    def project(l, t, source):
        mean = jnp.mean(source, axis=-1, keepdims=True)
        centred = source - mean
        var = jnp.mean(centred * centred, axis=-1, keepdims=True)
        g, b = gains[2 * l : 2 * l + 1, :], biases[2 * l : 2 * l + 1, :]
        n = (centred * lax.rsqrt(var + 1e-05) * g + b).astype(BF16)
        normed[pl.ds(t * 256, 256), :] = n
        mask = jnp.concatenate([chunk_mask(2 * t), chunk_mask(2 * t + 1)], axis=1)
        for side in range(2):
            value = dot(w_t[l, side * C : (side + 1) * C, :], n, NT)
            gated = dot(w_t[l, (side + 2) * C : (side + 3) * C, :], n, NT)
            res = value * jax.nn.sigmoid(gated) * mask
            for e in range(2):
                wide[pl.ds(side * 16 + 2 * t + e, C, stride=32), :] = res[:, e * C : (e + 1) * C]

    def pack_send():
        def one(g, carry):
            send[pl.ds(g * 8, 8)] = wide[pl.ds(g * 256, 256), :].astype(BF16).reshape(8, 32, C)
            return carry

        lax.fori_loop(0, ND // 8, one, 0, unroll=4)

    def send_out(l, recv):
        for g in range(GROUPS):
            def one(k, carry):
                peer = me ^ group_offset(g, k)
                pltpu.make_async_remote_copy(
                    src_ref=send.at[peer], dst_ref=recv.at[me],
                    send_sem=send_sems.at[l], recv_sem=recv_sems.at[l, g],
                    device_id=place(peer), device_id_type=MESH).start()
                return carry

            lax.fori_loop(1 if g == 0 else 0, MEMBERS, one, 0)
        recv[me] = send[me]

    def gates(l):
        def one(t, carry):
            rows = pl.ds(pl.multiple_of(t * 256, 256), 256)
            gate[rows, :] = jax.nn.sigmoid(dot(normed[rows, :], w_in[l, :, 4 * C :], NN))
            return carry
        lax.fori_loop(0, 8, one, 0, unroll=4)

    def wait_for(ref, count, sem):
        part = ref.at[pl.ds(0, count)]
        pltpu.make_async_copy(part, part, sem).wait()

    def combine(l, recv, ret):
        for g in range(GROUPS):
            wait_for(recv, MEMBERS - (g == 0), recv_sems.at[l, g])
            ra = (r ^ ((g // 2) * 4 + g % 2)) // 4 * 4 + (r ^ g) % 2
            for c in range(NC):
                t0 = recv[ra * NC + c].astype(F32)
                t1 = recv[(ra + 2) * NC + c].astype(F32)
                a = jnp.where(low, t0, pltpu.roll(t1, ROWS, 1)).astype(BF16)
                b = jnp.where(low, pltpu.roll(t0, ROWS, 1), t1).astype(BF16)
                lanes = slice(g * C, (g + 1) * C)
                m_left[c, 0:16, lanes] = a[0:16]
                m_left[c, 16:32, lanes] = b[0:16]
                m_right[c, 0:16, lanes] = a[16:32]
                m_right[c, 16:32, lanes] = b[16:32]
        left = m_left[...].reshape(512, 512)
        for step in range(4):
            if l == 0:
                a0, a1 = (q // 8 + step % 2) % 2, (q // 2 + step // 2) % 2
                rel = (a0 + r // 4) % 2 * 2 + (a1 + r) % 2
                right = m_right[:, :, pl.ds(pl.multiple_of(rel * C, C), C)].reshape(512, C)
                res = dot(right, left, TN)
                targets = [2 * (a0 * 4 + jh * 2 + a1) + jq for jh in range(2) for jq in range(2)]
            else:
                b = (q % 4) ^ step
                right = jnp.concatenate([m_right[b + 4 * m] for m in range(4)], axis=0)
                res = dot(right, left, NT)
                targets = [b + 4 * m for m in range(4)]
            for i, tq in enumerate(targets):
                for g in range(4):
                    if l == 0:
                        ra = (r ^ ((g // 2) * 4 + g % 2)) // 4 * 4 + (r ^ g) % 2
                        rb = ra + 2
                    else:
                        ra, rb = 2 * g, 2 * g + 1
                    x0 = res[i * 32 : i * 32 + 16, g * C : (g + 1) * C]
                    x1 = res[i * 32 + 16 : i * 32 + 32, g * C : (g + 1) * C]
                    back[ra * NC + tq] = jnp.where(low, x0, pltpu.roll(x1, ROWS, 1)).astype(BF16)
                    back[rb * NC + tq] = jnp.where(low, pltpu.roll(x0, ROWS, 1), x1).astype(BF16)

            def one(k, carry):
                k = (7 * k) % MEMBERS
                tr = r ^ (k % 8)
                kq = k // 8
                if l == 0:
                    tq = (a0 * 8 + a1 * 2) + (q ^ (kq // 2 * 4 + kq % 2)) % 8 // 4 * 4 + (q ^ kq) % 2
                else:
                    tq = (q ^ (kq * 4)) // 4 * 4 + b
                peer = tr * NC + tq

                @pl.when(peer != me)
                def _():
                    pltpu.make_async_remote_copy(
                        src_ref=back.at[peer], dst_ref=ret.at[me],
                        send_sem=back_sems.at[l], recv_sem=ret_sems.at[l],
                        device_id=place(peer), device_id_type=MESH).start()
                return carry

            lax.fori_loop(0, MEMBERS, one, 0)
        ret[me] = back[me]

    def finish(l, t):
        parts = []
        for e in range(2):
            v = stage[pl.ds(2 * t + e, C, stride=16), :]
            mean = jnp.mean(v, axis=0, keepdims=True)
            centred = v - mean
            var = jnp.mean(centred * centred, axis=0, keepdims=True)
            n = (centred * lax.rsqrt(var + 1e-05) * cols[l, 0] + cols[l, 1]).astype(BF16)
            parts.append(dot(n, w_out[l], TN))
        rows = pl.ds(pl.multiple_of(t * 256, 256), 256)
        return x[rows, :] + gate[rows, :] * jnp.concatenate(parts, axis=0)

    def receive(l, ret):
        wait_for(ret, ND - 1, ret_sems.at[l])
        wait_for(send, ND - 1, send_sems.at[l])
        wait_for(back, ND - 1, back_sems.at[l])

        def one(t, carry):
            stage[pl.ds(t * 256, 256), :] = ret[pl.ds(t * 16, 16)].astype(F32).reshape(256, C)
            return carry
        lax.fori_loop(0, 8, one, 0, unroll=4)

    def first(t, carry):
        pieces = [pair[pl.ds(h * 16 + 2 * t + e, ROWS, stride=COLS), :] for e in range(2) for h in range(2)]
        source = jnp.concatenate(pieces, axis=0)
        x[pl.ds(pl.multiple_of(t * 256, 256), 256), :] = source
        project(0, t, source)
        return carry

    lax.fori_loop(0, 8, first, 0, unroll=4)
    pack_send()
    gates(0)
    pl.semaphore_wait(barrier, ND - 1)
    send_out(0, recv0)
    combine(0, recv0, ret0)
    receive(0, ret0)

    def second(t, carry):
        source = finish(0, t)
        x[pl.ds(pl.multiple_of(t * 256, 256), 256), :] = source
        project(1, t, source)
        return carry

    lax.fori_loop(0, 8, second, 0, unroll=4)
    pack_send()
    send_out(1, recv1)
    gates(1)
    combine(1, recv1, ret1)
    receive(1, ret1)

    def third(t, carry):
        res = finish(1, t)
        for e in range(2):
            for h in range(2):
                at = (2 * e + h) * ROWS
                out[pl.ds(h * 16 + 2 * t + e, ROWS, stride=COLS), :] = res[at : at + ROWS]
        return carry

    lax.fori_loop(0, 8, third, 0, unroll=4)


def body(pair, token_mask, norm_gains, norm_biases, in_weights, out_weights):
    vmem = pl.BlockSpec(memory_space=pltpu.VMEM)
    hbm = pl.BlockSpec(memory_space=pltpu.HBM)
    res = pl.pallas_call(
        kernel,
        out_shape=jax.ShapeDtypeStruct((ROWS * COLS, C), F32),
        in_specs=[hbm, pl.BlockSpec(memory_space=pltpu.SMEM), vmem, vmem, vmem, hbm, hbm],
        out_specs=vmem,
        scratch_shapes=[
            pltpu.VMEM((2048, C), F32),
            pltpu.VMEM((2, C, 5 * C), BF16),
            pltpu.VMEM((2, C, C), BF16),
            pltpu.VMEM((2048, C), F32),
            pltpu.VMEM((2048, C), BF16),
            pltpu.VMEM((2048, C), F32),
            pltpu.VMEM((2, 4 * C, C), BF16),
            pltpu.VMEM((2, 2, C, C), F32),
            pltpu.VMEM((ND, 32, C), BF16),
            pltpu.VMEM((ND, 32, C), BF16),
            pltpu.VMEM((ND, 32, C), BF16),
            pltpu.VMEM((ND, 16, C), BF16),
            pltpu.VMEM((ND, 16, C), BF16),
            pltpu.VMEM((ND, 16, C), BF16),
            pltpu.VMEM((2048, C), F32),
            pltpu.VMEM((NC, 32, 512), BF16),
            pltpu.VMEM((NC, 32, 512), BF16),
            pltpu.VMEM((4096, C), F32),
            pltpu.SemaphoreType.DMA((3,)),
            pltpu.SemaphoreType.DMA((2,)),
            pltpu.SemaphoreType.DMA((2, GROUPS)),
            pltpu.SemaphoreType.DMA((2,)),
            pltpu.SemaphoreType.DMA((2,)),
        ],
        compiler_params=pltpu.CompilerParams(
            collective_id=0, has_side_effects=True, vmem_limit_bytes=48 << 20),
    )(
        pair.reshape(ROWS * COLS, C), token_mask, token_mask.reshape(4, C),
        norm_gains.reshape(4, C), norm_biases.reshape(4, C), in_weights, out_weights,
    )
    return res.reshape(ROWS, COLS, C)


def solution(mesh):
    placed = (P("row", "col", None), P(), P(), P(), P(), P())
    return jax.shard_map(
        body, mesh=mesh, in_specs=placed, out_specs=P("row", "col", None), check_vma=False
    )
```

time: 95.1 us -> 84.6 us (0.89)
  Pallas kernels: 90.2 us -> 79.6 us
    pallas_call x1, Pallas kernels: 90.2 us -> 79.6 us  [body(): pl.pallas_call(kernel, out_shape=jax.ShapeDtypeStruct((ROWS * COLS, C), F...]
where the time goes in v2:
time: 84.6 us; the launch traced here: 84.3 us
  Pallas kernels  79.6 us (94%)
  local copies, waits for them, and re-layouts  4.72 us (6%)
    pallas_call x1, Pallas kernels, body(): pl.pallas_call(kernel, out_shape=jax.ShapeDtypeStruct((ROWS * COLS, C), F...  79.6 us
    unnamed x13, local copies, waits for them, and re-layouts  4.72 us

profile of v2, /device:TPU:1, one launch (start us, length us, event | category | flops | bytes accessed | tf_op | source)
XLA Modules:
  0.0 84.3 jit_solution(15021410292237766540)
XLA Ops:
  0.0 0.0 copy-start.5
  0.0 0.0 copy-start.4
  0.0 0.0 copy-start.3
  0.0 0.7 copy-done.5
  0.7 0.0 copy-done.4
  0.7 0.0 copy-done.3
  0.7 0.0 copy-start
  0.7 1.2 %copy-done = f32[64,32,128]{2,1,0:T(8,128)S(1)} copy-done((f32[64,32,128]{2,1,0:T(8,128)S(1)}, f32[64,32,128]{2,1,0:T(8,128)}, u32[]{:S(2)}) %copy-start) | copy-done | bytes 1048600
  1.9 0.0 copy-start.1
  1.9 1.0 %copy-done.1 = bf16[2,128,640]{2,1,0:T(8,128)(2,1)S(1)} copy-done((bf16[2,128,640]{2,1,0:T(8,128)(2,1)S(1)}, bf16[2,128,640]{2,1,0:T(8,128)(2,1)}, u32[]{:S(2)}) %copy-start.1) | copy-done | bytes 327704
  2.9 0.0 copy-start.2
  2.9 0.8 copy-done.2
  3.8 79.6 %shard_map.64 = f32[2048,128]{1,0:T(8,128)S(1)} custom-call(f32[2048,128]{1,0:T(8,128)S(1)} %bitcast.6, s32[512]{0:T(512)S(1)} %copy-done.3, s32[4,128]{1,0:T(4,128)S(1)} %bitcast.7, f32[4,128]{1,0:T(4,128)S(1)} %bitcast.8, f32[4,128]{1,0:T(4,128)S(1)} %bitcast.9, bf16[2,128,640]{2,1,0:T(8,128)(2,1)S(1)} %copy-done.1, bf16[2,128,128]{2,1,0:T(8,128)(2,1)S(1)} %copy-done.2), custom_call_target="tpu_custom_call" | custom-call | tf_op jit(solution)/shard_map/pallas_call | solution.py:254
  83.4 1.0 %copy.8 = f32[64,32,128]{2,1,0:T(8,128)} copy(f32[64,32,128]{2,1,0:T(8,128)S(1)} %bitcast.5) | data formatting | bytes 2097152
Async XLA Ops:
  0.0 0.7 copy-start.5
  0.0 0.7 copy-start.4
  0.0 0.7 copy-start.3
  0.7 1.2 %copy-start = (f32[64,32,128]{2,1,0:T(8,128)S(1)}, f32[64,32,128]{2,1,0:T(8,128)}, u32[]{:S(2)}) copy-start(f32[64,32,128]{2,1,0:T(8,128)} %param.6) | copy-start | bytes 3145732
  1.9 1.0 %copy-start.1 = (bf16[2,128,640]{2,1,0:T(8,128)(2,1)S(1)}, bf16[2,128,640]{2,1,0:T(8,128)(2,1)}, u32[]{:S(2)}) copy-start(bf16[2,128,640]{2,1,0:T(8,128)(2,1)} %w_in_hbm.1) | copy-start | bytes 983044
  2.9 0.8 copy-start.2

commit v3 on v2

v3 whole, which is shorter than its diff:
```python
import jax
import jax.numpy as jnp
from jax import lax
from jax.experimental import pallas as pl
from jax.experimental.pallas import tpu as pltpu
from jax.sharding import PartitionSpec as P

MESH = pl.DeviceIdType.MESH
F32, BF16 = jnp.float32, jnp.bfloat16
C = 128
ROWS, COLS = 64, 32
NR, NC = 8, 16
ND = NR * NC
CHUNKS = 16
GROUPS = 4
MEMBERS = ND // GROUPS
TN = (((0,), (0,)), ((), ()))
NT = (((1,), (1,)), ((), ()))
NN = (((1,), (0,)), ((), ()))


def dot(a, b, dims):
    return lax.dot_general(a, b, dims, preferred_element_type=F32)


def place(device):
    return (device >> 4, device & 15)


def group_offset(g, k):
    k = (7 * k) % MEMBERS
    return (g // 2) * 64 + (g % 2) * 16 + (k // 16) * 32 + k % 16


def norm_rows(v, gain, bias):
    mean = jnp.mean(v, axis=0, keepdims=True)
    centred = v - mean
    var = jnp.mean(centred * centred, axis=0, keepdims=True)
    return (centred * lax.rsqrt(var + 1e-05) * gain + bias).astype(BF16)


def kernel(pair_hbm, mask_smem, mask_vmem, gains, biases, w_in_hbm, w_out_hbm, out,
           pair, w_in, w_out, x, x_pos, normed, gate, w_t, w_gate_t, w_out_t, mask, cols,
           send, recv0, recv1, back, ret0, ret1, stage, m_left, m_right, wide,
           load_sems, in_sems, send_sems, recv_sems, back_sems, ret_sems):
    r, q = lax.axis_index("row"), lax.axis_index("col")
    me = r * NC + q
    quarter = (r >> 2) * 2 + (r & 1)

    barrier = pltpu.get_barrier_semaphore()
    loads = [
        pltpu.make_async_copy(w_in_hbm, w_in, load_sems.at[0]),
        pltpu.make_async_copy(pair_hbm, pair, load_sems.at[1]),
        pltpu.make_async_copy(w_out_hbm, w_out, load_sems.at[2]),
    ]
    for load in loads:
        load.start()
    for o in [group_offset(0, k) for k in range(1, MEMBERS)] + [group_offset(g, 0) for g in range(1, GROUPS)]:
        pl.semaphore_signal(barrier, inc=1, device_id=place(me ^ o), device_id_type=MESH)

    low = lax.broadcasted_iota(jnp.int32, (1, C), 1) < ROWS
    pair_rows = mask_vmem[pl.ds(r >> 1, 1), :].astype(F32)
    turned = pltpu.roll(pair_rows, ROWS, 1)
    mine = jnp.where((r & 1) == 0, pair_rows, turned)
    row_mask = jnp.where(low, mine, pltpu.roll(mine, ROWS, 1))
    for s in range(CHUNKS):
        a = mask_smem[q * COLS + s].astype(F32)
        b = mask_smem[q * COLS + CHUNKS + s].astype(F32)
        mask[s // 2, :, (s % 2) * C : (s % 2 + 1) * C] = row_mask * jnp.where(low, a, b)

    for l in range(2):
        for i in range(2):
            cols[l, i, 0] = jnp.broadcast_to(gains[2 * l + i : 2 * l + i + 1, :], (C, C)).T
            cols[l, i, 1] = jnp.broadcast_to(biases[2 * l + i : 2 * l + i + 1, :], (C, C)).T

    def turn_weights(l):
        for part in range(4):
            t = w_in[l, :, part * C : (part + 1) * C].T
            for d in range(8):
                at = part * 32 + (d // 2 % 2) * 16
                w_t[l, (d // 4) * 2 + d % 2, at : at + 16, :] = t[d * 16 : (d + 1) * 16, :]

    def first(t):
        for e in range(2):
            s = 2 * t + e
            pieces = [pair[pl.ds(h * 16 + s, ROWS, stride=COLS), :] for h in range(2)]
            v = jnp.concatenate(pieces, axis=0).T
            x[s] = v
            normed[:, s * C : (s + 1) * C] = norm_rows(v, cols[0, 0, 0], cols[0, 0, 1])

    def project(l, g):
        part = quarter ^ g
        w = w_t[l, part]
        base = (g % 2) * 1024
        for t in range(8):
            res = dot(w, normed[:, t * 256 : (t + 1) * 256], NN)
            for side in range(2):
                value = res[side * 32 : (side + 1) * 32]
                gated = res[64 + side * 32 : 64 + (side + 1) * 32]
                both = value * jax.nn.sigmoid(gated) * mask[t]
                for e in range(2):
                    wide[pl.ds(base + side * 16 + 2 * t + e, 32, stride=32), :] = both[:, e * C : (e + 1) * C]
        for i in range(4):
            at = (part >> 1) * 64 + (part & 1) * 16 + (i // 2) * 32 + (i % 2) * 8
            rows = wide[base + i * 256 : base + (i + 1) * 256, :]
            send[pl.ds(at, 8)] = rows.astype(BF16).reshape(8, 32, C)

    def send_group(l, g, recv):
        for k in range(1 if g == 0 else 0, MEMBERS):
            peer = me ^ group_offset(g, k)
            pltpu.make_async_remote_copy(
                src_ref=send.at[peer], dst_ref=recv.at[me],
                send_sem=send_sems.at[l], recv_sem=recv_sems.at[l, g],
                device_id=place(peer), device_id_type=MESH).start()
        if g == 0:
            recv[me] = send[me]

    def wait_for(ref, count, sem):
        part = ref.at[pl.ds(0, count)]
        pltpu.make_async_copy(part, part, sem).wait()

    def rows_of(g):
        ra = (r ^ ((g // 2) * 4 + g % 2)) & 5
        return ra, ra + 2

    def combine(l, recv, ret):
        for g in range(GROUPS):
            wait_for(recv, MEMBERS - (g == 0), recv_sems.at[l, g])
            ra, rb = rows_of(g)
            for c in range(NC):
                t0 = recv[ra * NC + c].astype(F32)
                t1 = recv[rb * NC + c].astype(F32)
                a = jnp.where(low, t0, pltpu.roll(t1, ROWS, 1)).astype(BF16)
                b = jnp.where(low, pltpu.roll(t0, ROWS, 1), t1).astype(BF16)
                lanes = slice(g * C, (g + 1) * C)
                m_left[c, 0:16, lanes] = a[0:16]
                m_left[c, 16:32, lanes] = b[0:16]
                m_right[c, 0:16, lanes] = a[16:32]
                m_right[c, 16:32, lanes] = b[16:32]
        left = m_left[...].reshape(512, 512)
        for step in range(4):
            if l == 0:
                a0, a1 = (q >> 3) ^ (step % 2), ((q >> 1) & 1) ^ (step // 2)
                rel = (a0 ^ (r >> 2)) * 2 + (a1 ^ (r & 1))
                right = m_right[:, :, pl.ds(pl.multiple_of(rel * C, C), C)].reshape(512, C)
                res = dot(right, left, TN)
                targets = [a0 * 8 + jh * 4 + a1 * 2 + jq for jh in range(2) for jq in range(2)]
            else:
                b = (q & 3) ^ step
                right = jnp.concatenate([m_right[b + 4 * m] for m in range(4)], axis=0)
                res = dot(right, left, NT)
                targets = [b + 4 * m for m in range(4)]
            for i, tq in enumerate(targets):
                for g in range(4):
                    ra, rb = rows_of(g) if l == 0 else (2 * g, 2 * g + 1)
                    x0 = res[i * 32 : i * 32 + 16, g * C : (g + 1) * C]
                    x1 = res[i * 32 + 16 : i * 32 + 32, g * C : (g + 1) * C]
                    back[ra * NC + tq] = jnp.where(low, x0, pltpu.roll(x1, ROWS, 1)).astype(BF16)
                    back[rb * NC + tq] = jnp.where(low, pltpu.roll(x0, ROWS, 1), x1).astype(BF16)
            for k in range(MEMBERS):
                k = (7 * k) % MEMBERS
                kq = k // 8
                if l == 0:
                    o = (step % 2) * 8 + (step // 2) * 2 + (kq // 2) * 4 + kq % 2
                else:
                    o = kq * 4 + step
                o += (k % 8) * NC
                if o == 0:
                    continue
                peer = me ^ o
                pltpu.make_async_remote_copy(
                    src_ref=back.at[peer], dst_ref=ret.at[me],
                    send_sem=back_sems.at[l], recv_sem=ret_sems.at[l],
                    device_id=place(peer), device_id_type=MESH).start()
        ret[me] = back[me]

    def receive(l, ret):
        wait_for(ret, ND - 1, ret_sems.at[l])
        for t in range(8):
            stage[t * 256 : (t + 1) * 256, :] = ret[t * 16 : (t + 1) * 16].astype(F32).reshape(256, C)

    def normed_out(l, s):
        return norm_rows(stage[pl.ds(s, C, stride=16), :], cols[l, 1, 0], cols[l, 1, 1])

    loads[0].wait()
    turn_weights(0)
    loads[1].wait()
    for t in range(8):
        first(t)
    project(0, 0)
    pl.semaphore_wait(barrier, MEMBERS - 1 + GROUPS - 1)
    for g in range(1, GROUPS):
        pl.semaphore_signal(in_sems.at[g], inc=1, device_id=place(me ^ group_offset(g, 0)), device_id_type=MESH)
    send_group(0, 0, recv0)
    for g in range(1, GROUPS):
        project(0, g)
        pl.semaphore_wait(in_sems.at[g], 1)
        send_group(0, g, recv0)
    loads[2].wait()
    for l in range(2):
        w_out_t[l] = w_out[l].T
    w_gate_t[...] = w_in[0, :, 4 * C :].T
    for t in range(CHUNKS):
        gate[t] = jax.nn.sigmoid(dot(w_gate_t[...], normed[:, t * C : (t + 1) * C], NN))
    turn_weights(1)
    combine(0, recv0, ret0)
    wait_for(send, ND - 1, send_sems.at[0])
    receive(0, ret0)

    for s in range(CHUNKS):
        v = x[s] + gate[s] * dot(w_out_t[0], normed_out(0, s), NN)
        x[s] = v
        normed[:, s * C : (s + 1) * C] = norm_rows(v, cols[1, 0, 0], cols[1, 0, 1])
    for g in range(GROUPS):
        project(1, g)
        send_group(1, g, recv1)
    for s in range(CHUNKS):
        x_pos[s] = x[s].T
        gate[s] = jax.nn.sigmoid(dot(normed[:, s * C : (s + 1) * C], w_in[1, :, 4 * C :], TN))
    wait_for(back, ND - 1, back_sems.at[0])
    combine(1, recv1, ret1)
    wait_for(send, ND - 1, send_sems.at[1])
    receive(1, ret1)
    wait_for(back, ND - 1, back_sems.at[1])

    for s in range(CHUNKS):
        res = x_pos[s] + gate[s] * dot(normed_out(1, s), w_out[1], TN)
        for h in range(2):
            out[pl.ds(h * 16 + s, ROWS, stride=COLS), :] = res[h * ROWS : (h + 1) * ROWS]


def body(pair, token_mask, norm_gains, norm_biases, in_weights, out_weights):
    vmem = pl.BlockSpec(memory_space=pltpu.VMEM)
    hbm = pl.BlockSpec(memory_space=pltpu.HBM)
    res = pl.pallas_call(
        kernel,
        out_shape=jax.ShapeDtypeStruct((ROWS * COLS, C), F32),
        in_specs=[hbm, pl.BlockSpec(memory_space=pltpu.SMEM), vmem, vmem, vmem, hbm, hbm],
        out_specs=vmem,
        scratch_shapes=[
            pltpu.VMEM((2048, C), F32),
            pltpu.VMEM((2, C, 5 * C), BF16),
            pltpu.VMEM((2, C, C), BF16),
            pltpu.VMEM((CHUNKS, C, C), F32),
            pltpu.VMEM((CHUNKS, C, C), F32),
            pltpu.VMEM((C, 2048), BF16),
            pltpu.VMEM((CHUNKS, C, C), F32),
            pltpu.VMEM((2, GROUPS, C, C), BF16),
            pltpu.VMEM((C, C), BF16),
            pltpu.VMEM((2, C, C), BF16),
            pltpu.VMEM((8, 1, 256), F32),
            pltpu.VMEM((2, 2, 2, C, C), F32),
            pltpu.VMEM((ND, 32, C), BF16),
            pltpu.VMEM((ND, 32, C), BF16),
            pltpu.VMEM((ND, 32, C), BF16),
            pltpu.VMEM((ND, 16, C), BF16),
            pltpu.VMEM((ND, 16, C), BF16),
            pltpu.VMEM((ND, 16, C), BF16),
            pltpu.VMEM((2048, C), F32),
            pltpu.VMEM((NC, 32, 512), BF16),
            pltpu.VMEM((NC, 32, 512), BF16),
            pltpu.VMEM((2048, C), F32),
            pltpu.SemaphoreType.DMA((3,)),
            pltpu.SemaphoreType.REGULAR((GROUPS,)),
            pltpu.SemaphoreType.DMA((2,)),
            pltpu.SemaphoreType.DMA((2, GROUPS)),
            pltpu.SemaphoreType.DMA((2,)),
            pltpu.SemaphoreType.DMA((2,)),
        ],
        compiler_params=pltpu.CompilerParams(
            collective_id=0, has_side_effects=True, vmem_limit_bytes=48 << 20),
    )(
        pair.reshape(ROWS * COLS, C), token_mask, token_mask.reshape(4, C),
        norm_gains.reshape(4, C), norm_biases.reshape(4, C), in_weights, out_weights,
    )
    return res.reshape(ROWS, COLS, C)


def solution(mesh):
    placed = (P("row", "col", None), P(), P(), P(), P(), P())
    return jax.shard_map(
        body, mesh=mesh, in_specs=placed, out_specs=P("row", "col", None), check_vma=False
    )
```

time: 84.6 us -> 71.5 us (0.85)
  Pallas kernels: 79.6 us -> 66.5 us
    pallas_call x1, Pallas kernels: 79.6 us -> 66.5 us  [body(): pl.pallas_call(kernel, out_shape=jax.ShapeDtypeStruct((ROWS * COLS, C), F...]
where the time goes in v3:
time: 71.5 us; the launch traced here: 71.3 us
  Pallas kernels  66.5 us (93%)
  local copies, waits for them, and re-layouts  4.72 us (7%)
    pallas_call x1, Pallas kernels, body(): pl.pallas_call(kernel, out_shape=jax.ShapeDtypeStruct((ROWS * COLS, C), F...  66.5 us
    unnamed x13, local copies, waits for them, and re-layouts  4.72 us

profile of v3, /device:TPU:1, one launch (start us, length us, event | category | flops | bytes accessed | tf_op | source)
XLA Modules:
  0.0 71.3 jit_solution(3484252856741565777)
XLA Ops:
  0.0 0.0 copy-start.5
  0.0 0.0 copy-start.4
  0.0 0.0 copy-start.3
  0.0 0.7 copy-done.5
  0.7 0.0 copy-done.4
  0.7 0.0 copy-done.3
  0.7 0.0 copy-start
  0.7 1.2 %copy-done = f32[64,32,128]{2,1,0:T(8,128)S(1)} copy-done((f32[64,32,128]{2,1,0:T(8,128)S(1)}, f32[64,32,128]{2,1,0:T(8,128)}, u32[]{:S(2)}) %copy-start) | copy-done | bytes 1048600
  1.9 0.0 copy-start.1
  1.9 1.0 %copy-done.1 = bf16[2,128,640]{2,1,0:T(8,128)(2,1)S(1)} copy-done((bf16[2,128,640]{2,1,0:T(8,128)(2,1)S(1)}, bf16[2,128,640]{2,1,0:T(8,128)(2,1)}, u32[]{:S(2)}) %copy-start.1) | copy-done | bytes 327704
  2.9 0.0 copy-start.2
  2.9 0.8 %copy-done.2 = bf16[2,128,128]{2,1,0:T(8,128)(2,1)S(1)} copy-done((bf16[2,128,128]{2,1,0:T(8,128)(2,1)S(1)}, bf16[2,128,128]{2,1,0:T(8,128)(2,1)}, u32[]{:S(2)}) %copy-start.2) | copy-done | bytes 65560
  3.8 66.5 %shard_map.64 = f32[2048,128]{1,0:T(8,128)S(1)} custom-call(f32[2048,128]{1,0:T(8,128)S(1)} %bitcast.6, s32[512]{0:T(512)S(1)} %copy-done.3, s32[4,128]{1,0:T(4,128)S(1)} %bitcast.7, f32[4,128]{1,0:T(4,128)S(1)} %bitcast.8, f32[4,128]{1,0:T(4,128)S(1)} %bitcast.9, bf16[2,128,640]{2,1,0:T(8,128)(2,1)S(1)} %copy-done.1, bf16[2,128,128]{2,1,0:T(8,128)(2,1)S(1)} %copy-done.2), custom_call_target="tpu_custom_call" | custom-call | tf_op jit(solution)/shard_map/pallas_call | solution.py:235
  70.3 1.0 %copy.8 = f32[64,32,128]{2,1,0:T(8,128)} copy(f32[64,32,128]{2,1,0:T(8,128)S(1)} %bitcast.5) | data formatting | bytes 2097152
Async XLA Ops:
  0.0 0.7 copy-start.5
  0.0 0.7 copy-start.4
  0.0 0.7 copy-start.3
  0.7 1.2 %copy-start = (f32[64,32,128]{2,1,0:T(8,128)S(1)}, f32[64,32,128]{2,1,0:T(8,128)}, u32[]{:S(2)}) copy-start(f32[64,32,128]{2,1,0:T(8,128)} %param.6) | copy-start | bytes 3145732
  1.9 1.0 %copy-start.1 = (bf16[2,128,640]{2,1,0:T(8,128)(2,1)S(1)}, bf16[2,128,640]{2,1,0:T(8,128)(2,1)}, u32[]{:S(2)}) copy-start(bf16[2,128,640]{2,1,0:T(8,128)(2,1)} %w_in_hbm.1) | copy-start | bytes 983044
  2.9 0.8 %copy-start.2 = (bf16[2,128,128]{2,1,0:T(8,128)(2,1)S(1)}, bf16[2,128,128]{2,1,0:T(8,128)(2,1)}, u32[]{:S(2)}) copy-start(bf16[2,128,128]{2,1,0:T(8,128)(2,1)} %w_out_hbm.1) | copy-start | bytes 196612

commit v4 on v3

--- a/solution.py
+++ b/solution.py
@@ -27,9 +27,22 @@
     return (device >> 4, device & 15)
 
 
-def group_offset(g, k):
-    k = (7 * k) % MEMBERS
-    return (g // 2) * 64 + (g % 2) * 16 + (k // 16) * 32 + k % 16
+def hops(o):
+    return sum((0, 1, 2, 1)[(o >> hi & 1) * 2 + (o >> lo & 1)] for hi, lo in ((3, 6), (5, 4), (2, 1)))
+
+
+def group_bits(g):
+    return (g // 2) * 64 + (g % 2) * 16
+
+
+def far_first(offsets):
+    offsets = list(offsets)
+    mixed = [offsets[(7 * k) % len(offsets)] for k in range(len(offsets))]
+    return sorted(mixed, key=lambda o: -hops(o))
+
+
+def group_offsets(g):
+    return [o for o in far_first(group_bits(g) + (k // 16) * 32 + k % 16 for k in range(MEMBERS)) if o]
 
 
 def norm_rows(v, gain, bias):
@@ -39,8 +52,8 @@
     return (centred * lax.rsqrt(var + 1e-05) * gain + bias).astype(BF16)
 
 
-def kernel(pair_hbm, mask_smem, mask_vmem, gains, biases, w_in_hbm, w_out_hbm, out,
-           pair, w_in, w_out, x, x_pos, normed, gate, w_t, w_gate_t, w_out_t, mask, cols,
+def kernel(pair_hbm, mask_hbm, rows_hbm, gains_hbm, biases_hbm, w_in_hbm, w_out_hbm, out,
+           pair, mask_smem, mask_vmem, gains, biases, w_in, w_out, x, x_pos, normed, gate, w_t, w_gate_t, w_out_t, mask, cols,
            send, recv0, recv1, back, ret0, ret1, stage, m_left, m_right, wide,
            load_sems, in_sems, send_sems, recv_sems, back_sems, ret_sems):
     r, q = lax.axis_index("row"), lax.axis_index("col")
@@ -52,12 +65,18 @@
         pltpu.make_async_copy(w_in_hbm, w_in, load_sems.at[0]),
         pltpu.make_async_copy(pair_hbm, pair, load_sems.at[1]),
         pltpu.make_async_copy(w_out_hbm, w_out, load_sems.at[2]),
+        pltpu.make_async_copy(mask_hbm, mask_smem, load_sems.at[3]),
+        pltpu.make_async_copy(rows_hbm, mask_vmem, load_sems.at[4]),
+        pltpu.make_async_copy(gains_hbm, gains, load_sems.at[5]),
+        pltpu.make_async_copy(biases_hbm, biases, load_sems.at[6]),
     ]
     for load in loads:
         load.start()
-    for o in [group_offset(0, k) for k in range(1, MEMBERS)] + [group_offset(g, 0) for g in range(1, GROUPS)]:
+    for o in group_offsets(0) + [group_bits(g) for g in range(1, GROUPS)]:
         pl.semaphore_signal(barrier, inc=1, device_id=place(me ^ o), device_id_type=MESH)
 
+    for load in loads[3:]:
+        load.wait()
     low = lax.broadcasted_iota(jnp.int32, (1, C), 1) < ROWS
     pair_rows = mask_vmem[pl.ds(r >> 1, 1), :].astype(F32)
     turned = pltpu.roll(pair_rows, ROWS, 1)
@@ -106,8 +125,8 @@
             send[pl.ds(at, 8)] = rows.astype(BF16).reshape(8, 32, C)
 
     def send_group(l, g, recv):
-        for k in range(1 if g == 0 else 0, MEMBERS):
-            peer = me ^ group_offset(g, k)
+        for o in group_offsets(g):
+            peer = me ^ o
             pltpu.make_async_remote_copy(
                 src_ref=send.at[peer], dst_ref=recv.at[me],
                 send_sem=send_sems.at[l], recv_sem=recv_sems.at[l, g],
@@ -123,55 +142,76 @@
         ra = (r ^ ((g // 2) * 4 + g % 2)) & 5
         return ra, ra + 2
 
-    def combine(l, recv, ret):
+    def give_back(l, ret, peer):
+        pltpu.make_async_remote_copy(
+            src_ref=back.at[peer], dst_ref=ret.at[me],
+            send_sem=back_sems.at[l], recv_sem=ret_sems.at[l],
+            device_id=place(peer), device_id_type=MESH).start()
+
+    def assemble(l, recv, g):
+        wait_for(recv, MEMBERS - (g == 0), recv_sems.at[l, g])
+        ra, rb = rows_of(g)
+        lanes = slice(g * C, (g + 1) * C)
+        for c in range(NC):
+            t0 = recv[ra * NC + c].astype(F32)
+            t1 = recv[rb * NC + c].astype(F32)
+            a = jnp.where(low, t0, pltpu.roll(t1, ROWS, 1)).astype(BF16)
+            b = jnp.where(low, pltpu.roll(t0, ROWS, 1), t1).astype(BF16)
+            m_left[c, 0:16, lanes] = a[0:16]
+            m_left[c, 16:32, lanes] = b[0:16]
+            m_right[c, 0:16, lanes] = a[16:32]
+            m_right[c, 16:32, lanes] = b[16:32]
+
+    def pack(tile, ra, rb, tq):
+        x0, x1 = tile[0:16], tile[16:32]
+        back[ra * NC + tq] = jnp.where(low, x0, pltpu.roll(x1, ROWS, 1)).astype(BF16)
+        back[rb * NC + tq] = jnp.where(low, pltpu.roll(x0, ROWS, 1), x1).astype(BF16)
+
+    def combine_outgoing(recv, ret):
         for g in range(GROUPS):
-            wait_for(recv, MEMBERS - (g == 0), recv_sems.at[l, g])
-            ra, rb = rows_of(g)
-            for c in range(NC):
-                t0 = recv[ra * NC + c].astype(F32)
-                t1 = recv[rb * NC + c].astype(F32)
-                a = jnp.where(low, t0, pltpu.roll(t1, ROWS, 1)).astype(BF16)
-                b = jnp.where(low, pltpu.roll(t0, ROWS, 1), t1).astype(BF16)
-                lanes = slice(g * C, (g + 1) * C)
-                m_left[c, 0:16, lanes] = a[0:16]
-                m_left[c, 16:32, lanes] = b[0:16]
-                m_right[c, 0:16, lanes] = a[16:32]
-                m_right[c, 16:32, lanes] = b[16:32]
+            assemble(0, recv, g)
+            lanes = slice(g * C, (g + 1) * C)
+            right = m_right[:, :, lanes].reshape(512, C)
+            res = dot(right, m_left[:, :, : (g + 1) * C].reshape(512, (g + 1) * C), TN)
+            blocks = {(g, gi): res[:, gi * C : (gi + 1) * C] for gi in range(g + 1)}
+            if g:
+                left = m_left[:, :, lanes].reshape(512, C)
+                res = dot(m_right[:, :, : g * C].reshape(512, g * C), left, TN)
+                blocks.update({(gj, g): res[gj * C : (gj + 1) * C] for gj in range(g)})
+            sends = []
+            for (gj, gi), block in blocks.items():
+                jr, (ra, rb) = rows_of(gj)[0], rows_of(gi)
+                for jh in range(2):
+                    for jq in range(2):
+                        at = jh * 64 + jq * 32
+                        pack(block[at : at + 32], ra, rb, (jr >> 2) * 8 + jh * 4 + (jr & 1) * 2 + jq)
+                for zz in range(2):
+                    for yy in range(2):
+                        for jq in range(2):
+                            away = hops(group_bits(gi) + zz * 32) + yy
+                            tr = (r ^ ((gi // 2) * 4 + gi % 2)) ^ (zz * 2)
+                            tq = (jr >> 2) * 8 + ((q & 4) ^ (yy * 4)) + (jr & 1) * 2 + jq
+                            sends.append((away, tr * NC + tq))
+            for _, peer in sorted(sends, key=lambda e: -e[0]):
+                @pl.when(peer != me)
+                def _(peer=peer):
+                    give_back(0, ret, peer)
+        ret[me] = back[me]
+
+    def combine_incoming(recv, ret):
+        for g in range(GROUPS):
+            assemble(1, recv, g)
         left = m_left[...].reshape(512, 512)
         for step in range(4):
-            if l == 0:
-                a0, a1 = (q >> 3) ^ (step % 2), ((q >> 1) & 1) ^ (step // 2)
-                rel = (a0 ^ (r >> 2)) * 2 + (a1 ^ (r & 1))
-                right = m_right[:, :, pl.ds(pl.multiple_of(rel * C, C), C)].reshape(512, C)
-                res = dot(right, left, TN)
-                targets = [a0 * 8 + jh * 4 + a1 * 2 + jq for jh in range(2) for jq in range(2)]
-            else:
-                b = (q & 3) ^ step
-                right = jnp.concatenate([m_right[b + 4 * m] for m in range(4)], axis=0)
-                res = dot(right, left, NT)
-                targets = [b + 4 * m for m in range(4)]
-            for i, tq in enumerate(targets):
-                for g in range(4):
-                    ra, rb = rows_of(g) if l == 0 else (2 * g, 2 * g + 1)
-                    x0 = res[i * 32 : i * 32 + 16, g * C : (g + 1) * C]
-                    x1 = res[i * 32 + 16 : i * 32 + 32, g * C : (g + 1) * C]
-                    back[ra * NC + tq] = jnp.where(low, x0, pltpu.roll(x1, ROWS, 1)).astype(BF16)
-                    back[rb * NC + tq] = jnp.where(low, pltpu.roll(x0, ROWS, 1), x1).astype(BF16)
-            for k in range(MEMBERS):
-                k = (7 * k) % MEMBERS
-                kq = k // 8
-                if l == 0:
-                    o = (step % 2) * 8 + (step // 2) * 2 + (kq // 2) * 4 + kq % 2
-                else:
-                    o = kq * 4 + step
-                o += (k % 8) * NC
-                if o == 0:
-                    continue
-                peer = me ^ o
-                pltpu.make_async_remote_copy(
-                    src_ref=back.at[peer], dst_ref=ret.at[me],
-                    send_sem=back_sems.at[l], recv_sem=ret_sems.at[l],
-                    device_id=place(peer), device_id_type=MESH).start()
+            b = (q & 3) ^ step
+            right = jnp.concatenate([m_right[b + 4 * m] for m in range(4)], axis=0)
+            res = dot(right, left, NT)
+            for m in range(4):
+                for p in range(4):
+                    pack(res[m * 32 : (m + 1) * 32, p * C : (p + 1) * C], 2 * p, 2 * p + 1, b + 4 * m)
+            for o in far_first((k // 4) * NC + (k % 4) * 4 + step for k in range(MEMBERS)):
+                if o:
+                    give_back(1, ret, me ^ o)
         ret[me] = back[me]
 
     def receive(l, ret):
@@ -190,7 +230,7 @@
     project(0, 0)
     pl.semaphore_wait(barrier, MEMBERS - 1 + GROUPS - 1)
     for g in range(1, GROUPS):
-        pl.semaphore_signal(in_sems.at[g], inc=1, device_id=place(me ^ group_offset(g, 0)), device_id_type=MESH)
+        pl.semaphore_signal(in_sems.at[g], inc=1, device_id=place(me ^ group_bits(g)), device_id_type=MESH)
     send_group(0, 0, recv0)
     for g in range(1, GROUPS):
         project(0, g)
@@ -203,7 +243,7 @@
     for t in range(CHUNKS):
         gate[t] = jax.nn.sigmoid(dot(w_gate_t[...], normed[:, t * C : (t + 1) * C], NN))
     turn_weights(1)
-    combine(0, recv0, ret0)
+    combine_outgoing(recv0, ret0)
     wait_for(send, ND - 1, send_sems.at[0])
     receive(0, ret0)
 
@@ -218,7 +258,7 @@
         x_pos[s] = x[s].T
         gate[s] = jax.nn.sigmoid(dot(normed[:, s * C : (s + 1) * C], w_in[1, :, 4 * C :], TN))
     wait_for(back, ND - 1, back_sems.at[0])
-    combine(1, recv1, ret1)
+    combine_incoming(recv1, ret1)
     wait_for(send, ND - 1, send_sems.at[1])
     receive(1, ret1)
     wait_for(back, ND - 1, back_sems.at[1])
@@ -235,10 +275,14 @@
     res = pl.pallas_call(
         kernel,
         out_shape=jax.ShapeDtypeStruct((ROWS * COLS, C), F32),
-        in_specs=[hbm, pl.BlockSpec(memory_space=pltpu.SMEM), vmem, vmem, vmem, hbm, hbm],
+        in_specs=[hbm] * 7,
         out_specs=vmem,
         scratch_shapes=[
             pltpu.VMEM((2048, C), F32),
+            pltpu.SMEM((512,), jnp.int32),
+            pltpu.VMEM((4, C), jnp.int32),
+            pltpu.VMEM((4, C), F32),
+            pltpu.VMEM((4, C), F32),
             pltpu.VMEM((2, C, 5 * C), BF16),
             pltpu.VMEM((2, C, C), BF16),
             pltpu.VMEM((CHUNKS, C, C), F32),
@@ -260,7 +304,7 @@
             pltpu.VMEM((NC, 32, 512), BF16),
             pltpu.VMEM((NC, 32, 512), BF16),
             pltpu.VMEM((2048, C), F32),
-            pltpu.SemaphoreType.DMA((3,)),
+            pltpu.SemaphoreType.DMA((7,)),
             pltpu.SemaphoreType.REGULAR((GROUPS,)),
             pltpu.SemaphoreType.DMA((2,)),
             pltpu.SemaphoreType.DMA((2, GROUPS)),

time: 71.5 us -> 69 us (0.965)
  Pallas kernels: 66.5 us -> 64 us
    pallas_call x1, Pallas kernels: 66.5 us -> 64 us  [body(): pl.pallas_call(kernel, out_shape=jax.ShapeDtypeStruct((ROWS * COLS, C), F...]
where the time goes in v4:
time: 69 us; the launch traced here: 68.8 us
  Pallas kernels  64 us (93%)
  local copies, waits for them, and re-layouts  4.72 us (7%)
    pallas_call x1, Pallas kernels, body(): pl.pallas_call(kernel, out_shape=jax.ShapeDtypeStruct((ROWS * COLS, C), F...  64 us
    unnamed x13, local copies, waits for them, and re-layouts  4.72 us

profile of v4, /device:TPU:1, one launch (start us, length us, event | category | flops | bytes accessed | tf_op | source)
XLA Modules:
  0.0 68.8 jit_solution(9139777917166162085)
XLA Ops:
  0.0 0.0 copy-start.5
  0.0 0.0 copy-start.4
  0.0 0.0 copy-start.3
  0.0 0.7 copy-done.5
  0.7 0.0 copy-done.4
  0.7 0.0 copy-done.3
  0.7 0.0 copy-start
  0.7 1.2 %copy-done = f32[64,32,128]{2,1,0:T(8,128)S(1)} copy-done((f32[64,32,128]{2,1,0:T(8,128)S(1)}, f32[64,32,128]{2,1,0:T(8,128)}, u32[]{:S(2)}) %copy-start) | copy-done | bytes 1048600
  1.9 0.0 copy-start.1
  1.9 1.0 %copy-done.1 = bf16[2,128,640]{2,1,0:T(8,128)(2,1)S(1)} copy-done((bf16[2,128,640]{2,1,0:T(8,128)(2,1)S(1)}, bf16[2,128,640]{2,1,0:T(8,128)(2,1)}, u32[]{:S(2)}) %copy-start.1) | copy-done | bytes 327704
  2.9 0.0 copy-start.2
  2.9 0.8 %copy-done.2 = bf16[2,128,128]{2,1,0:T(8,128)(2,1)S(1)} copy-done((bf16[2,128,128]{2,1,0:T(8,128)(2,1)S(1)}, bf16[2,128,128]{2,1,0:T(8,128)(2,1)}, u32[]{:S(2)}) %copy-start.2) | copy-done | bytes 65560
  3.8 64.0 %shard_map.64 = f32[2048,128]{1,0:T(8,128)S(1)} custom-call(f32[2048,128]{1,0:T(8,128)S(1)} %bitcast.6, s32[512]{0:T(512)S(1)} %copy-done.3, s32[4,128]{1,0:T(4,128)S(1)} %bitcast.7, f32[4,128]{1,0:T(4,128)S(1)} %bitcast.8, f32[4,128]{1,0:T(4,128)S(1)} %bitcast.9, bf16[2,128,640]{2,1,0:T(8,128)(2,1)S(1)} %copy-done.1, bf16[2,128,128]{2,1,0:T(8,128)(2,1)S(1)} %copy-done.2), custom_call_target="tpu_custom_call" | custom-call | tf_op jit(solution)/shard_map/pallas_call | solution.py:275
  67.8 1.0 %copy.8 = f32[64,32,128]{2,1,0:T(8,128)} copy(f32[64,32,128]{2,1,0:T(8,128)S(1)} %bitcast.5) | data formatting | bytes 2097152
Async XLA Ops:
  0.0 0.7 copy-start.5
  0.0 0.7 %copy-start.4 = (f32[2,2,128]{2,1,0:T(2,128)S(1)}, f32[2,2,128]{2,1,0:T(2,128)}, u32[]{:S(2)}) copy-start(f32[2,2,128]{2,1,0:T(2,128)} %param.8) | copy-start | bytes 6148
  0.0 0.7 %copy-start.3 = (s32[512]{0:T(512)S(1)}, s32[512]{0:T(512)}, u32[]{:S(2)}) copy-start(s32[512]{0:T(512)} %mask_hbm.1) | copy-start | bytes 6148
  0.7 1.2 %copy-start = (f32[64,32,128]{2,1,0:T(8,128)S(1)}, f32[64,32,128]{2,1,0:T(8,128)}, u32[]{:S(2)}) copy-start(f32[64,32,128]{2,1,0:T(8,128)} %param.6) | copy-start | bytes 3145732
  1.9 1.0 %copy-start.1 = (bf16[2,128,640]{2,1,0:T(8,128)(2,1)S(1)}, bf16[2,128,640]{2,1,0:T(8,128)(2,1)}, u32[]{:S(2)}) copy-start(bf16[2,128,640]{2,1,0:T(8,128)(2,1)} %w_in_hbm.1) | copy-start | bytes 983044
  2.9 0.8 %copy-start.2 = (bf16[2,128,128]{2,1,0:T(8,128)(2,1)S(1)}, bf16[2,128,128]{2,1,0:T(8,128)(2,1)}, u32[]{:S(2)}) copy-start(bf16[2,128,128]{2,1,0:T(8,128)(2,1)} %w_out_hbm.1) | copy-start | bytes 196612

commit v5 on v4

--- a/solution.py
+++ b/solution.py
@@ -41,8 +41,20 @@
     return sorted(mixed, key=lambda o: -hops(o))
 
 
-def group_offsets(g):
-    return [o for o in far_first(group_bits(g) + (k // 16) * 32 + k % 16 for k in range(MEMBERS)) if o]
+def group_offsets(l, g):
+    if l == 0:
+        members = [group_bits(g) + (k // 16) * 32 + k % 16 for k in range(MEMBERS)]
+    else:
+        members = [(k // 4) * 16 + (k // 2 % 2) * 8 + (k // 2 % 2 ^ g % 2) * 4 + (g // 2) * 2 + k % 2
+                   for k in range(MEMBERS)]
+    return [o for o in far_first(members) if o]
+
+
+def slot(l, d):
+    if l == 0:
+        return d
+    b = ((d >> 3) ^ (d >> 2)) & 1
+    return ((d >> 1) & 1) * 64 + b * 32 + (d >> 4) * 4 + ((d >> 3) & 1) * 2 + (d & 1)
 
 
 def norm_rows(v, gain, bias):
@@ -58,7 +70,8 @@
            load_sems, in_sems, send_sems, recv_sems, back_sems, ret_sems):
     r, q = lax.axis_index("row"), lax.axis_index("col")
     me = r * NC + q
-    quarter = (r >> 2) * 2 + (r & 1)
+    b0, y0 = ((q >> 3) ^ (q >> 2)) & 1, (q >> 1) & 1
+    quarters = ((r >> 2) * 2 + (r & 1), y0 * 2 + b0)
 
     barrier = pltpu.get_barrier_semaphore()
     loads = [
@@ -72,7 +85,7 @@
     ]
     for load in loads:
         load.start()
-    for o in group_offsets(0) + [group_bits(g) for g in range(1, GROUPS)]:
+    for o in group_offsets(0, 0) + [group_bits(g) for g in range(1, GROUPS)]:
         pl.semaphore_signal(barrier, inc=1, device_id=place(me ^ o), device_id_type=MESH)
 
     for load in loads[3:]:
@@ -87,17 +100,21 @@
         b = mask_smem[q * COLS + CHUNKS + s].astype(F32)
         mask[s // 2, :, (s % 2) * C : (s % 2 + 1) * C] = row_mask * jnp.where(low, a, b)
 
-    for l in range(2):
-        for i in range(2):
+    def turn_norm(l, i):
+        if True:
             cols[l, i, 0] = jnp.broadcast_to(gains[2 * l + i : 2 * l + i + 1, :], (C, C)).T
             cols[l, i, 1] = jnp.broadcast_to(biases[2 * l + i : 2 * l + i + 1, :], (C, C)).T
 
     def turn_weights(l):
         for part in range(4):
             t = w_in[l, :, part * C : (part + 1) * C].T
-            for d in range(8):
-                at = part * 32 + (d // 2 % 2) * 16
-                w_t[l, (d // 4) * 2 + d % 2, at : at + 16, :] = t[d * 16 : (d + 1) * 16, :]
+            if l == 0:
+                for d in range(8):
+                    at = part * 32 + (d // 2 % 2) * 16
+                    w_t[l, (d // 4) * 2 + d % 2, at : at + 16, :] = t[d * 16 : (d + 1) * 16, :]
+            else:
+                for g in range(4):
+                    w_t[l, g, part * 32 : (part + 1) * 32, :] = t[g * 32 : (g + 1) * 32, :]
 
     def first(t):
         for e in range(2):
@@ -108,7 +125,7 @@
             normed[:, s * C : (s + 1) * C] = norm_rows(v, cols[0, 0, 0], cols[0, 0, 1])
 
     def project(l, g):
-        part = quarter ^ g
+        part = quarters[l] ^ g
         w = w_t[l, part]
         base = (g % 2) * 1024
         for t in range(8):
@@ -120,19 +137,22 @@
                 for e in range(2):
                     wide[pl.ds(base + side * 16 + 2 * t + e, 32, stride=32), :] = both[:, e * C : (e + 1) * C]
         for i in range(4):
-            at = (part >> 1) * 64 + (part & 1) * 16 + (i // 2) * 32 + (i % 2) * 8
+            if l == 0:
+                at = (part >> 1) * 64 + (part & 1) * 16 + (i // 2) * 32 + (i % 2) * 8
+            else:
+                at = part * 32 + i * 8
             rows = wide[base + i * 256 : base + (i + 1) * 256, :]
             send[pl.ds(at, 8)] = rows.astype(BF16).reshape(8, 32, C)
 
-    def send_group(l, g, recv):
-        for o in group_offsets(g):
+    def send_groups(l, groups, recv):
+        for o, g in sorted([(o, g) for g in groups for o in group_offsets(l, g)], key=lambda e: -hops(e[0])):
             peer = me ^ o
             pltpu.make_async_remote_copy(
-                src_ref=send.at[peer], dst_ref=recv.at[me],
+                src_ref=send.at[slot(l, peer)], dst_ref=recv.at[me],
                 send_sem=send_sems.at[l], recv_sem=recv_sems.at[l, g],
                 device_id=place(peer), device_id_type=MESH).start()
-        if g == 0:
-            recv[me] = send[me]
+        if 0 in groups:
+            recv[me] = send[slot(l, me)]
 
     def wait_for(ref, count, sem):
         part = ref.at[pl.ds(0, count)]
@@ -144,23 +164,19 @@
 
     def give_back(l, ret, peer):
         pltpu.make_async_remote_copy(
-            src_ref=back.at[peer], dst_ref=ret.at[me],
+            src_ref=back.at[peer], dst_ref=ret.at[slot(l, me)],
             send_sem=back_sems.at[l], recv_sem=ret_sems.at[l],
             device_id=place(peer), device_id_type=MESH).start()
 
-    def assemble(l, recv, g):
-        wait_for(recv, MEMBERS - (g == 0), recv_sems.at[l, g])
-        ra, rb = rows_of(g)
-        lanes = slice(g * C, (g + 1) * C)
-        for c in range(NC):
-            t0 = recv[ra * NC + c].astype(F32)
-            t1 = recv[rb * NC + c].astype(F32)
-            a = jnp.where(low, t0, pltpu.roll(t1, ROWS, 1)).astype(BF16)
-            b = jnp.where(low, pltpu.roll(t0, ROWS, 1), t1).astype(BF16)
-            m_left[c, 0:16, lanes] = a[0:16]
-            m_left[c, 16:32, lanes] = b[0:16]
-            m_right[c, 0:16, lanes] = a[16:32]
-            m_right[c, 16:32, lanes] = b[16:32]
+    def assemble(recv, ra, rb, c, at, lanes):
+        t0 = recv[ra * NC + c].astype(F32)
+        t1 = recv[rb * NC + c].astype(F32)
+        a = jnp.where(low, t0, pltpu.roll(t1, ROWS, 1)).astype(BF16)
+        b = jnp.where(low, pltpu.roll(t0, ROWS, 1), t1).astype(BF16)
+        m_left[at, 0:16, lanes] = a[0:16]
+        m_left[at, 16:32, lanes] = b[0:16]
+        m_right[at, 0:16, lanes] = a[16:32]
+        m_right[at, 16:32, lanes] = b[16:32]
 
     def pack(tile, ra, rb, tq):
         x0, x1 = tile[0:16], tile[16:32]
@@ -169,8 +185,11 @@
 
     def combine_outgoing(recv, ret):
         for g in range(GROUPS):
-            assemble(0, recv, g)
+            wait_for(recv, MEMBERS - (g == 0), recv_sems.at[0, g])
             lanes = slice(g * C, (g + 1) * C)
+            ra, rb = rows_of(g)
+            for c in range(NC):
+                assemble(recv, ra, rb, c, c, lanes)
             right = m_right[:, :, lanes].reshape(512, C)
             res = dot(right, m_left[:, :, : (g + 1) * C].reshape(512, (g + 1) * C), TN)
             blocks = {(g, gi): res[:, gi * C : (gi + 1) * C] for gi in range(g + 1)}
@@ -178,41 +197,56 @@
                 left = m_left[:, :, lanes].reshape(512, C)
                 res = dot(m_right[:, :, : g * C].reshape(512, g * C), left, TN)
                 blocks.update({(gj, g): res[gj * C : (gj + 1) * C] for gj in range(g)})
-            sends = []
             for (gj, gi), block in blocks.items():
                 jr, (ra, rb) = rows_of(gj)[0], rows_of(gi)
                 for jh in range(2):
                     for jq in range(2):
                         at = jh * 64 + jq * 32
                         pack(block[at : at + 32], ra, rb, (jr >> 2) * 8 + jh * 4 + (jr & 1) * 2 + jq)
-                for zz in range(2):
-                    for yy in range(2):
-                        for jq in range(2):
-                            away = hops(group_bits(gi) + zz * 32) + yy
-                            tr = (r ^ ((gi // 2) * 4 + gi % 2)) ^ (zz * 2)
-                            tq = (jr >> 2) * 8 + ((q & 4) ^ (yy * 4)) + (jr & 1) * 2 + jq
-                            sends.append((away, tr * NC + tq))
+        for o in far_first(range(1, ND)):
+            give_back(0, ret, me ^ o)
+        ret[me] = back[me]
+
+    def combine_incoming(recv, ret):
+        def label(g):
+            return b0 ^ (g % 2), y0 ^ (g // 2)
+
+        def column(g, x, core):
+            b, y = label(g)
+            return x * 8 + (b ^ x) * 4 + y * 2 + core
+
+        for g in range(GROUPS):
+            wait_for(recv, MEMBERS - (g == 0), recv_sems.at[1, g])
+            for x in range(2):
+                for core in range(2):
+                    for p in range(4):
+                        assemble(recv, 2 * p, 2 * p + 1, column(g, x, core), g * 4 + x * 2 + core,
+                                 slice(p * C, (p + 1) * C))
+            right = m_right[g * 4 : (g + 1) * 4].reshape(C, 512)
+            res = dot(right, m_left[: (g + 1) * 4].reshape((g + 1) * C, 512), NT)
+            blocks = {(g, gi): res[:, gi * C : (gi + 1) * C] for gi in range(g + 1)}
+            if g:
+                left = m_left[g * 4 : (g + 1) * 4].reshape(C, 512)
+                res = dot(m_right[: g * 4].reshape(g * C, 512), left, NT)
+                blocks.update({(gj, g): res[gj * C : (gj + 1) * C] for gj in range(g)})
+            sends = []
+            for (gj, gi), block in blocks.items():
+                b, y = label(gi)
+                for x in range(2):
+                    for core in range(2):
+                        at = (x * 2 + core) * 32
+                        pack(block[at : at + 32], b * 2 + y, 4 + (b ^ 1) * 2 + y, column(gj, x, core))
+                for xr in range(2):
+                    tr = (r >> 2) ^ xr
+                    tr = tr * 4 + (tr ^ b) * 2 + y
+                    for k in range(4):
+                        o = (k // 2) * 8 + (k // 2 ^ gj % 2) * 4 + (gj // 2) * 2 + k % 2
+                        sends.append((hops(o & 6) + k // 2, tr * NC + (q ^ o)))
             for _, peer in sorted(sends, key=lambda e: -e[0]):
                 @pl.when(peer != me)
                 def _(peer=peer):
-                    give_back(0, ret, peer)
-        ret[me] = back[me]
-
-    def combine_incoming(recv, ret):
-        for g in range(GROUPS):
-            assemble(1, recv, g)
-        left = m_left[...].reshape(512, 512)
-        for step in range(4):
-            b = (q & 3) ^ step
-            right = jnp.concatenate([m_right[b + 4 * m] for m in range(4)], axis=0)
-            res = dot(right, left, NT)
-            for m in range(4):
-                for p in range(4):
-                    pack(res[m * 32 : (m + 1) * 32, p * C : (p + 1) * C], 2 * p, 2 * p + 1, b + 4 * m)
-            for o in far_first((k // 4) * NC + (k % 4) * 4 + step for k in range(MEMBERS)):
-                if o:
-                    give_back(1, ret, me ^ o)
-        ret[me] = back[me]
+                    give_back(1, ret, peer)
+        ret[slot(1, me)] = back[me]
 
     def receive(l, ret):
         wait_for(ret, ND - 1, ret_sems.at[l])
@@ -222,6 +256,7 @@
     def normed_out(l, s):
         return norm_rows(stage[pl.ds(s, C, stride=16), :], cols[l, 1, 0], cols[l, 1, 1])
 
+    turn_norm(0, 0)
     loads[0].wait()
     turn_weights(0)
     loads[1].wait()
@@ -231,12 +266,14 @@
     pl.semaphore_wait(barrier, MEMBERS - 1 + GROUPS - 1)
     for g in range(1, GROUPS):
         pl.semaphore_signal(in_sems.at[g], inc=1, device_id=place(me ^ group_bits(g)), device_id_type=MESH)
-    send_group(0, 0, recv0)
+    send_groups(0, (0,), recv0)
     for g in range(1, GROUPS):
         project(0, g)
         pl.semaphore_wait(in_sems.at[g], 1)
-        send_group(0, g, recv0)
+        send_groups(0, (g,), recv0)
     loads[2].wait()
+    for l, i in ((0, 1), (1, 0), (1, 1)):
+        turn_norm(l, i)
     for l in range(2):
         w_out_t[l] = w_out[l].T
     w_gate_t[...] = w_in[0, :, 4 * C :].T
@@ -251,9 +288,10 @@
         v = x[s] + gate[s] * dot(w_out_t[0], normed_out(0, s), NN)
         x[s] = v
         normed[:, s * C : (s + 1) * C] = norm_rows(v, cols[1, 0, 0], cols[1, 0, 1])
-    for g in range(GROUPS):
+    for g in range(0, GROUPS, 2):
         project(1, g)
-        send_group(1, g, recv1)
+        project(1, g + 1)
+        send_groups(1, (g, g + 1), recv1)
     for s in range(CHUNKS):
         x_pos[s] = x[s].T
         gate[s] = jax.nn.sigmoid(dot(normed[:, s * C : (s + 1) * C], w_in[1, :, 4 * C :], TN))

time: 69 us -> 67.9 us (0.984)
  Pallas kernels: 64 us -> 62.9 us
    pallas_call x1, Pallas kernels: 64 us -> 62.9 us  [body(): pl.pallas_call(kernel, out_shape=jax.ShapeDtypeStruct((ROWS * COLS, C), F...]
where the time goes in v5:
time: 67.9 us; the launch traced here: 67.7 us
  Pallas kernels  62.9 us (93%)
  local copies, waits for them, and re-layouts  4.72 us (7%)
    pallas_call x1, Pallas kernels, body(): pl.pallas_call(kernel, out_shape=jax.ShapeDtypeStruct((ROWS * COLS, C), F...  62.9 us
    unnamed x13, local copies, waits for them, and re-layouts  4.72 us

profile of v5, /device:TPU:1, one launch (start us, length us, event | category | flops | bytes accessed | tf_op | source)
XLA Modules:
  0.0 67.7 jit_solution(8592087774579742514)
XLA Ops:
  0.0 0.0 copy-start.5
  0.0 0.0 copy-start.4
  0.0 0.0 copy-start.3
  0.0 0.7 copy-done.5
  0.7 0.0 copy-done.4
  0.7 0.0 copy-done.3
  0.7 0.0 copy-start
  0.7 1.2 %copy-done = f32[64,32,128]{2,1,0:T(8,128)S(1)} copy-done((f32[64,32,128]{2,1,0:T(8,128)S(1)}, f32[64,32,128]{2,1,0:T(8,128)}, u32[]{:S(2)}) %copy-start) | copy-done | bytes 1048600
  1.9 0.0 copy-start.1
  1.9 1.0 %copy-done.1 = bf16[2,128,640]{2,1,0:T(8,128)(2,1)S(1)} copy-done((bf16[2,128,640]{2,1,0:T(8,128)(2,1)S(1)}, bf16[2,128,640]{2,1,0:T(8,128)(2,1)}, u32[]{:S(2)}) %copy-start.1) | copy-done | bytes 327704
  2.9 0.0 copy-start.2
  2.9 0.8 %copy-done.2 = bf16[2,128,128]{2,1,0:T(8,128)(2,1)S(1)} copy-done((bf16[2,128,128]{2,1,0:T(8,128)(2,1)S(1)}, bf16[2,128,128]{2,1,0:T(8,128)(2,1)}, u32[]{:S(2)}) %copy-start.2) | copy-done | bytes 65560
  3.8 62.9 %shard_map.64 = f32[2048,128]{1,0:T(8,128)S(1)} custom-call(f32[2048,128]{1,0:T(8,128)S(1)} %bitcast.6, s32[512]{0:T(512)S(1)} %copy-done.3, s32[4,128]{1,0:T(4,128)S(1)} %bitcast.7, f32[4,128]{1,0:T(4,128)S(1)} %bitcast.8, f32[4,128]{1,0:T(4,128)S(1)} %bitcast.9, bf16[2,128,640]{2,1,0:T(8,128)(2,1)S(1)} %copy-done.1, bf16[2,128,128]{2,1,0:T(8,128)(2,1)S(1)} %copy-done.2), custom_call_target="tpu_custom_call" | custom-call | tf_op jit(solution)/shard_map/pallas_call | solution.py:313
  66.7 1.0 %copy.8 = f32[64,32,128]{2,1,0:T(8,128)} copy(f32[64,32,128]{2,1,0:T(8,128)S(1)} %bitcast.5) | data formatting | bytes 2097152
Async XLA Ops:
  0.0 0.7 %copy-start.5 = (f32[2,2,128]{2,1,0:T(2,128)S(1)}, f32[2,2,128]{2,1,0:T(2,128)}, u32[]{:S(2)}) copy-start(f32[2,2,128]{2,1,0:T(2,128)} %param.9) | copy-start | bytes 6148
  0.0 0.7 %copy-start.4 = (f32[2,2,128]{2,1,0:T(2,128)S(1)}, f32[2,2,128]{2,1,0:T(2,128)}, u32[]{:S(2)}) copy-start(f32[2,2,128]{2,1,0:T(2,128)} %param.8) | copy-start | bytes 6148
  0.0 0.7 %copy-start.3 = (s32[512]{0:T(512)S(1)}, s32[512]{0:T(512)}, u32[]{:S(2)}) copy-start(s32[512]{0:T(512)} %mask_hbm.1) | copy-start | bytes 6148
  0.7 1.2 %copy-start = (f32[64,32,128]{2,1,0:T(8,128)S(1)}, f32[64,32,128]{2,1,0:T(8,128)}, u32[]{:S(2)}) copy-start(f32[64,32,128]{2,1,0:T(8,128)} %param.6) | copy-start | bytes 3145732
  1.9 1.0 %copy-start.1 = (bf16[2,128,640]{2,1,0:T(8,128)(2,1)S(1)}, bf16[2,128,640]{2,1,0:T(8,128)(2,1)}, u32[]{:S(2)}) copy-start(bf16[2,128,640]{2,1,0:T(8,128)(2,1)} %w_in_hbm.1) | copy-start | bytes 983044
  2.9 0.8 %copy-start.2 = (bf16[2,128,128]{2,1,0:T(8,128)(2,1)S(1)}, bf16[2,128,128]{2,1,0:T(8,128)(2,1)}, u32[]{:S(2)}) copy-start(bf16[2,128,128]{2,1,0:T(8,128)(2,1)} %w_out_hbm.1) | copy-start | bytes 196612

commit v6 on v5

--- a/solution.py
+++ b/solution.py
@@ -37,7 +37,7 @@
 
 def far_first(offsets):
     offsets = list(offsets)
-    mixed = [offsets[(7 * k) % len(offsets)] for k in range(len(offsets))]
+    mixed = [offsets[(5 * k) % len(offsets)] for k in range(len(offsets))]
     return sorted(mixed, key=lambda o: -hops(o))
 
 
@@ -267,10 +267,14 @@
     for g in range(1, GROUPS):
         pl.semaphore_signal(in_sems.at[g], inc=1, device_id=place(me ^ group_bits(g)), device_id_type=MESH)
     send_groups(0, (0,), recv0)
-    for g in range(1, GROUPS):
-        project(0, g)
-        pl.semaphore_wait(in_sems.at[g], 1)
-        send_groups(0, (g,), recv0)
+    project(0, 1)
+    pl.semaphore_wait(in_sems.at[1], 1)
+    send_groups(0, (1,), recv0)
+    project(0, 2)
+    project(0, 3)
+    pl.semaphore_wait(in_sems.at[2], 1)
+    pl.semaphore_wait(in_sems.at[3], 1)
+    send_groups(0, (2, 3), recv0)
     loads[2].wait()
     for l, i in ((0, 1), (1, 0), (1, 1)):
         turn_norm(l, i)

time: 67.9 us -> 67.4 us (level)
  no operation moved by 1% of the time
where the time goes in v6:
time: 67.4 us; the launch traced here: 67.2 us
  Pallas kernels  62.5 us (93%)
  local copies, waits for them, and re-layouts  4.72 us (7%)
    pallas_call x1, Pallas kernels, body(): pl.pallas_call(kernel, out_shape=jax.ShapeDtypeStruct((ROWS * COLS, C), F...  62.5 us
    unnamed x13, local copies, waits for them, and re-layouts  4.72 us

profile of v6, /device:TPU:1, one launch (start us, length us, event | category | flops | bytes accessed | tf_op | source)
XLA Modules:
  0.0 67.2 jit_solution(2133971923247595779)
XLA Ops:
  0.0 0.0 copy-start.5
  0.0 0.0 copy-start.4
  0.0 0.0 copy-start.3
  0.0 0.7 %copy-done.5 = f32[2,2,128]{2,1,0:T(2,128)S(1)} copy-done((f32[2,2,128]{2,1,0:T(2,128)S(1)}, f32[2,2,128]{2,1,0:T(2,128)}, u32[]{:S(2)}) %copy-start.5) | copy-done | bytes 2072
  0.7 0.0 copy-done.4
  0.7 0.0 copy-done.3
  0.7 0.0 copy-start
  0.7 1.2 %copy-done = f32[64,32,128]{2,1,0:T(8,128)S(1)} copy-done((f32[64,32,128]{2,1,0:T(8,128)S(1)}, f32[64,32,128]{2,1,0:T(8,128)}, u32[]{:S(2)}) %copy-start) | copy-done | bytes 1048600
  1.9 0.0 copy-start.1
  1.9 1.0 %copy-done.1 = bf16[2,128,640]{2,1,0:T(8,128)(2,1)S(1)} copy-done((bf16[2,128,640]{2,1,0:T(8,128)(2,1)S(1)}, bf16[2,128,640]{2,1,0:T(8,128)(2,1)}, u32[]{:S(2)}) %copy-start.1) | copy-done | bytes 327704
  2.9 0.0 copy-start.2
  2.9 0.8 %copy-done.2 = bf16[2,128,128]{2,1,0:T(8,128)(2,1)S(1)} copy-done((bf16[2,128,128]{2,1,0:T(8,128)(2,1)S(1)}, bf16[2,128,128]{2,1,0:T(8,128)(2,1)}, u32[]{:S(2)}) %copy-start.2) | copy-done | bytes 65560
  3.8 62.5 %shard_map.64 = f32[2048,128]{1,0:T(8,128)S(1)} custom-call(f32[2048,128]{1,0:T(8,128)S(1)} %bitcast.6, s32[512]{0:T(512)S(1)} %copy-done.3, s32[4,128]{1,0:T(4,128)S(1)} %bitcast.7, f32[4,128]{1,0:T(4,128)S(1)} %bitcast.8, f32[4,128]{1,0:T(4,128)S(1)} %bitcast.9, bf16[2,128,640]{2,1,0:T(8,128)(2,1)S(1)} %copy-done.1, bf16[2,128,128]{2,1,0:T(8,128)(2,1)S(1)} %copy-done.2), custom_call_target="tpu_custom_call" | custom-call | tf_op jit(solution)/shard_map/pallas_call | solution.py:317
  66.2 1.0 %copy.8 = f32[64,32,128]{2,1,0:T(8,128)} copy(f32[64,32,128]{2,1,0:T(8,128)S(1)} %bitcast.5) | data formatting | bytes 2097152
Async XLA Ops:
  0.0 0.7 %copy-start.5 = (f32[2,2,128]{2,1,0:T(2,128)S(1)}, f32[2,2,128]{2,1,0:T(2,128)}, u32[]{:S(2)}) copy-start(f32[2,2,128]{2,1,0:T(2,128)} %param.9) | copy-start | bytes 6148
  0.0 0.7 %copy-start.4 = (f32[2,2,128]{2,1,0:T(2,128)S(1)}, f32[2,2,128]{2,1,0:T(2,128)}, u32[]{:S(2)}) copy-start(f32[2,2,128]{2,1,0:T(2,128)} %param.8) | copy-start | bytes 6148
  0.0 0.7 %copy-start.3 = (s32[512]{0:T(512)S(1)}, s32[512]{0:T(512)}, u32[]{:S(2)}) copy-start(s32[512]{0:T(512)} %mask_hbm.1) | copy-start | bytes 6148
  0.7 1.2 %copy-start = (f32[64,32,128]{2,1,0:T(8,128)S(1)}, f32[64,32,128]{2,1,0:T(8,128)}, u32[]{:S(2)}) copy-start(f32[64,32,128]{2,1,0:T(8,128)} %param.6) | copy-start | bytes 3145732
  1.9 1.0 %copy-start.1 = (bf16[2,128,640]{2,1,0:T(8,128)(2,1)S(1)}, bf16[2,128,640]{2,1,0:T(8,128)(2,1)}, u32[]{:S(2)}) copy-start(bf16[2,128,640]{2,1,0:T(8,128)(2,1)} %w_in_hbm.1) | copy-start | bytes 983044
  2.9 0.8 %copy-start.2 = (bf16[2,128,128]{2,1,0:T(8,128)(2,1)S(1)}, bf16[2,128,128]{2,1,0:T(8,128)(2,1)}, u32[]{:S(2)}) copy-start(bf16[2,128,128]{2,1,0:T(8,128)(2,1)} %w_out_hbm.1) | copy-start | bytes 196612

commit v7 on v6

--- a/solution.py
+++ b/solution.py
@@ -292,10 +292,11 @@
         v = x[s] + gate[s] * dot(w_out_t[0], normed_out(0, s), NN)
         x[s] = v
         normed[:, s * C : (s + 1) * C] = norm_rows(v, cols[1, 0, 0], cols[1, 0, 1])
-    for g in range(0, GROUPS, 2):
+    project(1, 0)
+    send_groups(1, (0,), recv1)
+    for g in range(1, GROUPS):
         project(1, g)
-        project(1, g + 1)
-        send_groups(1, (g, g + 1), recv1)
+    send_groups(1, (1, 2, 3), recv1)
     for s in range(CHUNKS):
         x_pos[s] = x[s].T
         gate[s] = jax.nn.sigmoid(dot(normed[:, s * C : (s + 1) * C], w_in[1, :, 4 * C :], TN))

time: 67.4 us -> 67.5 us (level)
  no operation moved by 1% of the time
where the time goes in v7:
time: 67.5 us; the launch traced here: 67.2 us
  Pallas kernels  62.5 us (93%)
  local copies, waits for them, and re-layouts  4.72 us (7%)
    pallas_call x1, Pallas kernels, body(): pl.pallas_call(kernel, out_shape=jax.ShapeDtypeStruct((ROWS * COLS, C), F...  62.5 us
    unnamed x13, local copies, waits for them, and re-layouts  4.72 us

profile of v7, /device:TPU:1, one launch (start us, length us, event | category | flops | bytes accessed | tf_op | source)
XLA Modules:
  0.0 67.2 jit_solution(3302669667209654933)
XLA Ops:
  0.0 0.0 copy-start.5
  0.0 0.0 copy-start.4
  0.0 0.0 copy-start.3
  0.0 0.7 %copy-done.5 = f32[2,2,128]{2,1,0:T(2,128)S(1)} copy-done((f32[2,2,128]{2,1,0:T(2,128)S(1)}, f32[2,2,128]{2,1,0:T(2,128)}, u32[]{:S(2)}) %copy-start.5) | copy-done | bytes 2072
  0.7 0.0 copy-done.4
  0.7 0.0 copy-done.3
  0.7 0.0 copy-start
  0.7 1.2 %copy-done = f32[64,32,128]{2,1,0:T(8,128)S(1)} copy-done((f32[64,32,128]{2,1,0:T(8,128)S(1)}, f32[64,32,128]{2,1,0:T(8,128)}, u32[]{:S(2)}) %copy-start) | copy-done | bytes 1048600
  1.9 0.0 copy-start.1
  1.9 1.0 %copy-done.1 = bf16[2,128,640]{2,1,0:T(8,128)(2,1)S(1)} copy-done((bf16[2,128,640]{2,1,0:T(8,128)(2,1)S(1)}, bf16[2,128,640]{2,1,0:T(8,128)(2,1)}, u32[]{:S(2)}) %copy-start.1) | copy-done | bytes 327704
  2.9 0.0 copy-start.2
  2.9 0.8 %copy-done.2 = bf16[2,128,128]{2,1,0:T(8,128)(2,1)S(1)} copy-done((bf16[2,128,128]{2,1,0:T(8,128)(2,1)S(1)}, bf16[2,128,128]{2,1,0:T(8,128)(2,1)}, u32[]{:S(2)}) %copy-start.2) | copy-done | bytes 65560
  3.8 62.5 %shard_map.64 = f32[2048,128]{1,0:T(8,128)S(1)} custom-call(f32[2048,128]{1,0:T(8,128)S(1)} %bitcast.6, s32[512]{0:T(512)S(1)} %copy-done.3, s32[4,128]{1,0:T(4,128)S(1)} %bitcast.7, f32[4,128]{1,0:T(4,128)S(1)} %bitcast.8, f32[4,128]{1,0:T(4,128)S(1)} %bitcast.9, bf16[2,128,640]{2,1,0:T(8,128)(2,1)S(1)} %copy-done.1, bf16[2,128,128]{2,1,0:T(8,128)(2,1)S(1)} %copy-done.2), custom_call_target="tpu_custom_call" | custom-call | tf_op jit(solution)/shard_map/pallas_call | solution.py:318
  66.2 1.0 %copy.8 = f32[64,32,128]{2,1,0:T(8,128)} copy(f32[64,32,128]{2,1,0:T(8,128)S(1)} %bitcast.5) | data formatting | bytes 2097152
Async XLA Ops:
  0.0 0.7 %copy-start.5 = (f32[2,2,128]{2,1,0:T(2,128)S(1)}, f32[2,2,128]{2,1,0:T(2,128)}, u32[]{:S(2)}) copy-start(f32[2,2,128]{2,1,0:T(2,128)} %param.9) | copy-start | bytes 6148
  0.0 0.7 %copy-start.4 = (f32[2,2,128]{2,1,0:T(2,128)S(1)}, f32[2,2,128]{2,1,0:T(2,128)}, u32[]{:S(2)}) copy-start(f32[2,2,128]{2,1,0:T(2,128)} %param.8) | copy-start | bytes 6148
  0.0 0.7 %copy-start.3 = (s32[512]{0:T(512)S(1)}, s32[512]{0:T(512)}, u32[]{:S(2)}) copy-start(s32[512]{0:T(512)} %mask_hbm.1) | copy-start | bytes 6148
  0.7 1.2 %copy-start = (f32[64,32,128]{2,1,0:T(8,128)S(1)}, f32[64,32,128]{2,1,0:T(8,128)}, u32[]{:S(2)}) copy-start(f32[64,32,128]{2,1,0:T(8,128)} %param.6) | copy-start | bytes 3145732
  1.9 1.0 %copy-start.1 = (bf16[2,128,640]{2,1,0:T(8,128)(2,1)S(1)}, bf16[2,128,640]{2,1,0:T(8,128)(2,1)}, u32[]{:S(2)}) copy-start(bf16[2,128,640]{2,1,0:T(8,128)(2,1)} %w_in_hbm.1) | copy-start | bytes 983044
  2.9 0.8 %copy-start.2 = (bf16[2,128,128]{2,1,0:T(8,128)(2,1)S(1)}, bf16[2,128,128]{2,1,0:T(8,128)(2,1)}, u32[]{:S(2)}) copy-start(bf16[2,128,128]{2,1,0:T(8,128)(2,1)} %w_out_hbm.1) | copy-start | bytes 196612
